TPU v7x, 256 devices: a whole 4x4x8 slice. The times are simulated.
256 devices in a mesh: row: 8 (over x, core), col: 32 (over z, y).
Axes of the slice: x: 4, y: 4, z: 8, core: 2. Of those that a mesh axis runs over, the one named last changes fastest.
Arguments:
- acts: bfloat16 [2048, 16384], P('row', 'col'), may hold values from -8 to 8
- sample_idx: int32 [8, 96], P('row'), may hold values from 0 to 255
- sample_count: int32 [8], replicated, may hold values from 1 to 96, 256 in all
- codes: bfloat16 [16384, 16384], P('row', 'col'), may hold values from -127 to 127, as said below
- scales: float32 [256, 16384], P('row', 'col'), may hold values from 4e-05 to 0.00016
- grad: bfloat16 [16384, 8192], P('row', 'col'), may hold values from -6 to 6
Outputs:
- new_ema: bfloat16 [16384, 16384], P('row', 'col')
- factor_step: float32 [16384, 16384], P('row', 'col')
- solved: float32 [16384, 8192], P('row', 'col')
Inputs may be any that keep to these rules, and one draw needn't show every extreme that they name: `sample_count`: the counts sum to 256; the largest is 96. `sample_idx`: entries k at or past sample_count[g] of row g are unused. `codes`: whole numbers.
All inputs are finite; a program needn't handle non-finite values.
Results may differ from a plain program's by a relative error of at most 0.0056.
Values may be sent and summed in bfloat16 or wider, within the bound.
No kernel may reach another device: no remote copies, remote signals or barrier semaphores. Data moves between devices by JAX's collectives and lax.ppermute only.
A program may use at most 64 MiB of HBM per device.

v0:
```python
import jax
import jax.numpy as jnp
from jax import lax
from jax.sharding import PartitionSpec as P

P_SIZE = 256


ema_decay = 0.95
damping = 1.0


def broadcast(value, axis, source):
    kept = jnp.where(lax.axis_index(axis) == source, value, 0).astype(value.dtype)
    return lax.psum(kept, axis)


def on_device(acts, sample_idx, sample_count, codes, scales, grad):
    rows_here = codes.shape[0]
    tile_width = codes.shape[1]
    grad_width = grad.shape[1]
    row_count = lax.axis_size("row")
    col_count = lax.axis_size("col")
    per_row = col_count // row_count
    row_id = lax.axis_index("row")
    col_id = lax.axis_index("col")
    capacity = sample_idx.shape[1]
    total_rows = row_count * capacity // 3
    block_rows = rows_here // scales.shape[0]
    slot_index = jnp.arange(capacity, dtype=jnp.int32)
    count_here = lax.dynamic_index_in_dim(sample_count, row_id, keepdims=False)
    picked = jnp.take(acts, sample_idx[0], axis=0)
    masked = jnp.where(slot_index[:, None] < count_here, picked, jnp.zeros_like(picked))
    gathered = lax.all_gather(masked, "row", axis=0, tiled=True)
    feature_parts = [
        broadcast(gathered, "col", row_id * per_row + piece_index) for piece_index in range(per_row)
    ]
    feature_rows = jnp.concatenate(feature_parts, axis=1)
    product = lax.dot_general(
        feature_rows, gathered, (((0,), (0,)), ((), ())), preferred_element_type=jnp.float32
    )
    old_ema = (
        codes.astype(jnp.float32).reshape(rows_here // block_rows, block_rows, tile_width)
        * scales[:, None, :]
    ).reshape(rows_here, tile_width)
    new_ema = (ema_decay * old_ema + (1.0 - ema_decay) / total_rows * product).astype(jnp.bfloat16)
    glob_rows = row_id * rows_here + jnp.arange(rows_here, dtype=jnp.int32)[:, None]
    glob_cols = col_id * tile_width + jnp.arange(tile_width, dtype=jnp.int32)[None, :]
    full_tile = new_ema.astype(jnp.float32) + damping * (glob_rows == glob_cols)
    piece_width = min(tile_width, P_SIZE)
    panel_parts = broadcast(new_ema[:, :piece_width], "col", 0)
    panel_input = panel_parts.astype(jnp.float32) + damping * (
        glob_rows == jnp.arange(P_SIZE, dtype=jnp.int32)[None, :]
    )
    identity = jnp.eye(P_SIZE, dtype=jnp.float32)
    own_block = jnp.where(row_id == 0, panel_input[:P_SIZE], identity)
    lead_factor = broadcast(jnp.linalg.cholesky(own_block), "row", 0)
    grad_lead = grad[:P_SIZE].astype(jnp.float32)
    panel = lax.linalg.triangular_solve(
        lead_factor, panel_input, left_side=False, lower=True, transpose_a=True
    )
    lead_solution = lax.linalg.triangular_solve(lead_factor, grad_lead, left_side=True, lower=True)
    leading = broadcast(lead_solution.astype(jnp.bfloat16), "row", 0).astype(lead_solution.dtype)
    column_rows = lax.dynamic_slice_in_dim(panel, col_id % per_row * tile_width, tile_width, 0)
    panel_cols = broadcast(column_rows.astype(jnp.bfloat16), "row", col_id // per_row).astype(
        column_rows.dtype
    )
    trailing = full_tile - jnp.dot(panel, panel_cols.T, precision=lax.Precision.HIGHEST)
    panel_here = jnp.concatenate(
        [panel, jnp.zeros((rows_here, tile_width - P_SIZE), jnp.float32)], axis=1
    )
    lower_part = jnp.where(glob_rows >= glob_cols, panel_here, 0.0)
    upper_part = jnp.where(glob_rows < P_SIZE, 0.0, trailing)
    factor_step = jnp.where(glob_cols < P_SIZE, lower_part, upper_part)
    remainder = grad.astype(jnp.float32) - jnp.dot(panel, leading, precision=lax.Precision.HIGHEST)
    leading_wide = jnp.concatenate(
        [leading, jnp.zeros((rows_here - P_SIZE, grad_width), jnp.float32)], axis=0
    )
    solved = jnp.where(glob_rows < P_SIZE, leading_wide, remainder)
    return (new_ema, factor_step, solved)


def solution(mesh):
    in_specs = (
        P("row", "col"),
        P("row", None),
        P(),
        P("row", "col"),
        P("row", "col"),
        P("row", "col"),
    )
    out_specs = (P("row", "col"), P("row", "col"), P("row", "col"))
    return jax.shard_map(
        on_device, mesh=mesh, in_specs=in_specs, out_specs=out_specs, check_vma=False
    )
```

profile of v0, /device:TPU:7, one launch (start us, length us, event | category | flops | bytes accessed | tf_op | source)
XLA Modules:
  0.0 582.7 jit_solution(14077643562308655878)
XLA Ops:
  11.4 14.0 %all_gather.3 = bf16[768,512]{1,0:T(8,128)(2,1)S(1)} all-gather(bf16[96,512]{1,0:T(8,128)(2,1)S(1)} %select_select_fusion.1), channel_id=1, replica_groups=mesh['row'=8,'col'=32] {'row'}, dimensions={0}, use_global_device_ids=true | all-gather | bytes 884736 | tf_op jit(solution)/shard_map/all_gather | solution.py:34
  25.3 1.8 broadcast_select_fusion.3
  27.2 2.5 mul.38
  29.7 5.5 copy.26
  35.3 2.4 copy.25
  37.6 146.4 %all-reduce.13.cloned.1.call-done = (bf16[768,512]{1,0:T(8,128)(2,1)}, bf16[768,512]{1,0:T(8,128)(2,1)}, bf16[768,512]{1,0:T(8,128)(2,1)}, bf16[768,512]{1,0:T(8,128)(2,1)}) async-done(((bf16[768,512]{1,0:T(8,128)(2,1)}, bf16[768,512]{1,0:T(8,128)(2,1)}, bf16[768,512]{1,0:T(8,128)(2,1)}, bf16[768,512]{1,0:T(8,128)(2,1)}), (bf16[768,512]{1,0:T(8,128)(2,1)}, bf16[768,512]{1,0:T(8,128)(2,1)}, ...) | async-done | bytes 3145744 | tf_op jit(solution)/shard_map/psum | solution.py:15
  184.0 6.0 %add_convert_fusion = bf16[2048,512]{0,1:T(8,128)(2,1)S(1)} fusion(f32[2048,512]{0,1:T(8,128)} %copy.26, bf16[2048,512]{0,1:T(8,128)(2,1)} %copy.25, bf16[768,512]{1,0:T(8,128)(2,1)S(1)} %all_gather.3, bf16[768,512]{1,0:T(8,128)(2,1)} %get-tuple-element.33, bf16[768,512]{1,0:T(8,128)(2,1)} %get-tuple-element.34, bf16[768,512]{1,0:T(8,128)(2,1)} %get-tuple-element.35, ...), kind=kOutput, calls=%fused_computation.5 | convolution fusion | flops 1629487104 | bytes 12320768 | tf_op jit(solution)/shard_map/dot_general | solution.py:39
  192.7 146.0 %all-reduce.9.cloned.1.call-done = bf16[2048,256]{0,1:T(8,128)(2,1)} async-done(((bf16[2048,256]{0,1:T(8,128)(2,1)}), bf16[2048,256]{0,1:T(8,128)(2,1)}) %all-reduce.9.cloned.1.call-update) | async-done | bytes 1048592 | tf_op jit(solution)/shard_map/psum | solution.py:15
  341.0 1.8 copy.28
  344.5 11.7 %cholesky.50 = f32[128,128]{1,0:T(8,128)S(1)} custom-call(f32[128,128]{1,0:T(8,128)S(1)} %cholesky.118), custom_call_target="Cholesky" | custom-call | tf_op jit(solution)/shard_map/jit(cholesky)/cholesky | solution.py:57
  356.8 10.6 %custom-call.16 = f32[1,128,128]{1,2,0:T(8,128)S(1)} custom-call(f32[1,128,128]{2,1,0:T(8,128)} %get-tuple-element.46), custom_call_target="InvertDiagBlocksLowerTriangular" | custom-call | tf_op jit(solution)/shard_map/jit(cholesky)/cholesky | solution.py:57
  368.5 1.7 convolution_subtract_fusion.3
  370.3 12.5 %cholesky.105 = f32[128,128]{1,0:T(8,128)S(1)} custom-call(f32[128,128]{1,0:T(8,128)} %convolution_subtract_fusion.3), custom_call_target="Cholesky" | custom-call | tf_op jit(solution)/shard_map/jit(cholesky)/cholesky | solution.py:57
  392.6 63.4 %all-reduce.11.cloned.1.call-done = f32[256,256]{0,1:T(8,128)} async-done(((f32[256,256]{0,1:T(8,128)}), f32[256,256]{0,1:T(8,128)}) %all-reduce.11.cloned.1.call-update) | async-done | bytes 262160 | tf_op jit(solution)/shard_map/psum | solution.py:15
  457.7 4.2 while.1
  461.9 19.7 %custom-call.17 = f32[2,128,128]{1,2,0:T(8,128)S(1)} custom-call(f32[2,128,128]{2,1,0:T(8,128)S(1)} %get-tuple-element.10), custom_call_target="InvertDiagBlocksLowerTriangular" | custom-call | tf_op jit(solution)/shard_map/triangular_solve | solution.py:59
  484.6 2.0 fusion.9
  487.9 1.9 convolution_subtract_fusion.1
  492.4 3.9 copy.38
  496.3 61.0 %all-reduce.15.cloned.1.call-done = (bf16[512,256]{0,1:T(8,128)(2,1)}, bf16[256,256]{0,1:T(8,128)(2,1)}) async-done(((bf16[512,256]{0,1:T(8,128)(2,1)}, bf16[256,256]{0,1:T(8,128)(2,1)}), (bf16[512,256]{0,1:T(8,128)(2,1)}, bf16[256,256]{0,1:T(8,128)(2,1)})) %all-reduce.15.cloned.1.call-update) | async-done | bytes 393232 | tf_op jit(solution)/shard_map/psum | solution.py:15
  557.3 3.7 fusion.8
  561.0 2.9 copy.40
  564.0 6.9 %fusion = f32[2048,512]{0,1:T(8,128)} fusion(f32[2048,128]{0,1:T(8,128)S(1)} %fusion.21, f32[2048,128]{0,1:T(8,128)S(1)} %fusion.9, bf16[2048,512]{0,1:T(8,128)(2,1)} %copy-done.1, bf16[512,256]{0,1:T(8,128)(2,1)S(1)} %copy-done.13, f32[512]{0:T(512)S(1)} %pad.11.clone, s32[2048]{0:T(1024)S(1)} %iota_add_fusion, s32[512]{0:T(512)S(1)} %iota_add_fusion.1, ...), kind=kOutput, calls=%fused_computation.4 | convolution fusion | flops 3233284096 | bytes 8665600 | tf_op jit(solution)/shard_map/dot_general | solution.py:68
  570.9 5.3 copy.39
  (87 shorter events, 33.6 us)
Async XLA Ops:
  7.2 3.3 copy-start
  7.2 176.9 %all-reduce.13.cloned.1.call-start = ((), (), s32[]{:S(2)}) async-start(), calls=%async_computation.2 | async-start | bytes 6291456 | tf_op jit(solution)/shard_map/psum | solution.py:15
  25.3 1.8 copy-start.12
  27.1 311.5 %all-reduce.9.cloned.1.call-start = ((), (), s32[]{:S(2)}) async-start(), calls=%async_computation | async-start | bytes 2097152 | tf_op jit(solution)/shard_map/psum | solution.py:15
  29.7 5.5 copy-start.3
  190.0 1.3 copy-start.1
  192.4 263.6 %all-reduce.11.cloned.1.call-start = ((), (), s32[]{:S(2)}) async-start(), calls=%async_computation.1 | async-start | bytes 524288 | tf_op jit(solution)/shard_map/psum | solution.py:15
  192.7 198.5 %copy-start.5 = (bf16[2048,256]{1,0:T(8,128)(2,1)S(1)}, bf16[2048,256]{1,0:T(8,128)(2,1)}, u32[]{:S(2)}) copy-start(bf16[2048,256]{1,0:T(8,128)(2,1)} %param.11) | copy-start | bytes 3145732
  343.7 0.7 copy-start.6
  356.2 0.7 copy-start.9
  382.8 0.6 copy-start.11
  390.3 167.0 %all-reduce.15.cloned.1.call-start = ((), (), s32[]{:S(2)}) async-start(), calls=%async_computation.3 | async-start | bytes 786432 | tf_op jit(solution)/shard_map/psum | solution.py:15
  461.9 22.0 %copy-start.4 = (f32[256,256]{0,1:T(8,128)}, f32[256,256]{0,1:T(8,128)S(1)}, u32[]{:S(2)}) copy-start(f32[256,256]{0,1:T(8,128)S(1)} %get-tuple-element.114) | copy-start | bytes 786436
  481.5 2.3 copy-start.7
  484.6 5.2 copy-start.8
  486.6 4.3 copy-start.10
  491.6 65.7 %copy-start.2 = (bf16[2048,256]{0,1:T(8,128)(2,1)S(1)}, bf16[2048,256]{0,1:T(8,128)(2,1)}, u32[]{:S(2)}) copy-start(bf16[2048,256]{0,1:T(8,128)(2,1)} %copy.36) | copy-start | bytes 3145732
  561.0 2.9 copy-start.13
Sparse Core Ops, SparseCore 0:
  27.3 156.7 all-reduce.12
  192.5 146.1 all-reduce.8
  390.5 65.4 all-reduce.10
  492.5 64.7 all-reduce.14
where the time goes:
time: 585 us; the launch traced here: 583 us
  waiting for transfers between devices  417 us (71%)
  other arithmetic  68.5 us (12%)
  local copies, waits for them, and re-layouts  39.6 us (7%)
  matrix products  27.9 us (5%)
  between operations  15.4 us (3%)
  blocking collectives  14 us (2%)
    psum x4, waiting for transfers between devices, broadcast(): return lax.psum(kept, axis)  417 us
    another operation x7, other arithmetic, on_device(): lead_factor = broadcast(jnp.linalg.cholesky(own_block), 'row', 0)  36.9 us
    another operation x3, other arithmetic, on_device(): lax.linalg.triangular_solve(lead_factor, panel_input, left_side=False, lo...  21.2 us
    unnamed x33, local copies, waits for them, and re-layouts  18.7 us
    all_gather x1, blocking collectives, on_device(): gathered = lax.all_gather(masked, 'row', axis=0, tiled=True)  14 us
  transfers between devices with their start and end apart: 4, of which 4 were waited for; matrix products, arithmetic and copies ran while one was open for 3% of the time, Pallas kernels for 0%

commit v1 on v0

v1 whole, which is shorter than its diff:
```python
import jax
import jax.numpy as jnp
from jax import lax
from jax.sharding import PartitionSpec as P

PANEL = 256
SAMPLES = 256

ema_decay = 0.95
damping = 1.0
update_weight = (1.0 - ema_decay) / SAMPLES
bf16 = jnp.bfloat16
f32 = jnp.float32
HIGHEST = lax.Precision.HIGHEST


def gram(a, b):
    return lax.dot_general(a, b, (((0,), (0,)), ((), ())), preferred_element_type=f32)


def on_device(acts, sample_idx, sample_count, codes, scales, grad):
    rows_here, width = codes.shape
    grad_width = grad.shape[1]
    row_n = lax.axis_size("row")
    col_n = lax.axis_size("col")
    y_n = col_n // row_n
    z_n = col_n // y_n
    row = lax.axis_index("row")
    col = lax.axis_index("col")
    y = col % y_n
    y_groups = [[z * y_n + i for i in range(y_n)] for z in range(z_n)]
    z_groups = [[z * y_n + i for z in range(z_n)] for i in range(y_n)]
    swap = [
        (g * col_n + y_n * r + j, r * col_n + y_n * g + j)
        for g in range(row_n)
        for r in range(row_n)
        for j in range(y_n)
    ]
    part = SAMPLES // row_n
    quarter = rows_here // y_n
    piece = quarter // z_n
    capacity = sample_idx.shape[1]
    block = rows_here // scales.shape[0]

    with jax.named_scope("pick_samples"):
        before = jnp.sum(jnp.where(jnp.arange(row_n) < row, sample_count, 0))
        count_here = lax.dynamic_index_in_dim(sample_count, row, keepdims=False)
        slot = jnp.arange(capacity, dtype=jnp.int32)
        place = jnp.arange(SAMPLES, dtype=jnp.int32)
        takes = (place[:, None] - before == slot[None, :]) & (slot[None, :] < count_here)
        holds = sample_idx[0][:, None] == jnp.arange(acts.shape[0], dtype=jnp.int32)[None, :]
        choice = jnp.dot(takes.astype(bf16), holds.astype(bf16), preferred_element_type=f32)
        placed = jnp.dot(choice.astype(bf16), acts, preferred_element_type=f32).astype(bf16)
    with jax.named_scope("old_panel"):
        old_panel = (
            ema_decay
            * (
                codes[:, :PANEL].astype(f32).reshape(rows_here // block, block, PANEL)
                * scales[:, None, :PANEL]
            )
        ).reshape(rows_here, PANEL).astype(bf16)
    with jax.named_scope("row_scatter"):
        outgoing = jnp.concatenate([placed, grad[:SAMPLES], old_panel[:PANEL]], axis=1)
        incoming = lax.all_to_all(outgoing, "row", 0, 0, tiled=True).reshape(row_n, part, -1)
        own_slice = jnp.sum(incoming[:, :, :width].astype(f32), axis=0).astype(bf16)
        grad_slice = incoming[0, :, width : width + grad_width]
        lead_slice = incoming[0, :, width + grad_width :]
    with jax.named_scope("y_scatter"):
        old_quarter = old_panel[:quarter]
        slices = jnp.concatenate([own_slice[:, :PANEL], lead_slice], axis=0)
        for d in range(1, y_n):
            moved = lax.ppermute(old_panel[d * quarter : (d + 1) * quarter], "col", [(0, d)])
            old_quarter = jnp.where(y == d, moved, old_quarter)
        sent = slices
        for d in range(1, y_n):
            moved = lax.ppermute(sent, "col", [(0, d)])
            slices = jnp.where(y == d, moved, slices)
    with jax.named_scope("z_scatter"):
        outgoing = jnp.concatenate(
            [
                old_quarter.reshape(z_n, piece, PANEL),
                jnp.broadcast_to(slices[None], (z_n,) + slices.shape),
            ],
            axis=1,
        )
        incoming = lax.all_to_all(
            outgoing, "col", 0, 0, tiled=True, axis_index_groups=z_groups
        )[0]
        old_piece = incoming[:piece]
        slices = incoming[piece:]
    with jax.named_scope("swap_samples"):
        swapped = lax.ppermute(own_slice, ("row", "col"), swap)
    halves = width // PANEL
    with jax.named_scope("row_gather"):
        outgoing = jnp.concatenate(
            [slices, grad_slice]
            + [own_slice[:, h * PANEL : (h + 1) * PANEL] for h in range(halves)],
            axis=0,
        )
        incoming = lax.all_to_all(
            jnp.broadcast_to(outgoing[None], (row_n,) + outgoing.shape), "row", 0, 0, tiled=True
        )
        x_lead, old_lead, grad_lead, *x_cols = [
            incoming[:, i * part : (i + 1) * part].reshape(SAMPLES, PANEL) for i in range(3 + halves)
        ]
    with jax.named_scope("z_gather"):
        outgoing = jnp.concatenate(
            [old_piece] + [swapped[:, h * PANEL : (h + 1) * PANEL] for h in range(halves)], axis=0
        )
        incoming = lax.all_to_all(
            jnp.broadcast_to(outgoing[None], (z_n,) + outgoing.shape),
            "col",
            0,
            0,
            tiled=True,
            axis_index_groups=z_groups,
        )
        old_quarter = incoming[:, :piece].reshape(quarter, PANEL)
        x_quarter = [
            incoming[:, piece + h * part : piece + (h + 1) * part].reshape(SAMPLES, PANEL)
            for h in range(halves)
        ]
    with jax.named_scope("swap_panel"):
        old_cols = lax.ppermute(old_quarter, ("row", "col"), swap)
    with jax.named_scope("y_gather"):
        outgoing = jnp.concatenate([old_quarter] + x_quarter, axis=0)
        incoming = lax.all_to_all(
            jnp.broadcast_to(outgoing[None], (y_n,) + outgoing.shape),
            "col",
            0,
            0,
            tiled=True,
            axis_index_groups=y_groups,
        )
        old_rows = incoming[:, :quarter].reshape(rows_here, PANEL)
        x_rows = jnp.concatenate(
            [
                incoming[i, quarter + h * SAMPLES : quarter + (h + 1) * SAMPLES]
                for i in range(y_n)
                for h in range(halves)
            ],
            axis=1,
        )
    x_cols = jnp.concatenate(x_cols, axis=1)

    eye = jnp.eye(PANEL, dtype=f32)
    glob_rows = row * rows_here + jnp.arange(rows_here, dtype=jnp.int32)[:, None]
    glob_cols = col * width + jnp.arange(width, dtype=jnp.int32)[None, :]

    def panel_ema(x, old):
        return (old.astype(f32) + update_weight * gram(x, x_lead)).astype(bf16).astype(f32)

    with jax.named_scope("factor"):
        lead = panel_ema(x_lead, old_lead) + damping * eye
        lower = jnp.linalg.cholesky(lead)
        inverse = lax.linalg.triangular_solve(lower, eye, left_side=True, lower=True)
        leading = jnp.dot(inverse, grad_lead.astype(f32), precision=HIGHEST)
    with jax.named_scope("panel_cols"):
        cols_in = panel_ema(x_cols, old_cols) + damping * (
            glob_cols.T == jnp.arange(PANEL, dtype=jnp.int32)[None, :]
        )
        panel_cols = jnp.dot(cols_in, inverse.T, precision=HIGHEST)
    with jax.named_scope("panel_rows"):
        rows_in = panel_ema(x_rows, old_rows) + damping * (
            glob_rows == jnp.arange(PANEL, dtype=jnp.int32)[None, :]
        )
        panel = jnp.dot(rows_in, inverse.T, precision=HIGHEST)
    with jax.named_scope("new_average"):
        old_ema = (
            codes.astype(f32).reshape(rows_here // block, block, width) * scales[:, None, :]
        ).reshape(rows_here, width)
        new_ema = (ema_decay * old_ema + update_weight * gram(x_rows, x_cols)).astype(bf16)
    with jax.named_scope("trailing"):
        full_tile = new_ema.astype(f32) + damping * (glob_rows == glob_cols)
        trailing = full_tile - jnp.dot(panel, panel_cols.T, precision=HIGHEST)
        panel_here = jnp.concatenate(
            [panel, jnp.zeros((rows_here, width - PANEL), f32)], axis=1
        )
        lower_part = jnp.where(glob_rows >= glob_cols, panel_here, 0.0)
        upper_part = jnp.where(glob_rows < PANEL, 0.0, trailing)
        factor_step = jnp.where(glob_cols < PANEL, lower_part, upper_part)
    with jax.named_scope("solved_rows"):
        remainder = grad.astype(f32) - jnp.dot(panel, leading, precision=HIGHEST)
        leading_wide = jnp.concatenate(
            [leading, jnp.zeros((rows_here - PANEL, grad_width), f32)], axis=0
        )
        solved = jnp.where(glob_rows < PANEL, leading_wide, remainder)
    return (new_ema, factor_step, solved)


def solution(mesh):
    in_specs = (
        P("row", "col"),
        P("row", None),
        P(),
        P("row", "col"),
        P("row", "col"),
        P("row", "col"),
    )
    out_specs = (P("row", "col"), P("row", "col"), P("row", "col"))
    return jax.shard_map(
        on_device, mesh=mesh, in_specs=in_specs, out_specs=out_specs, check_vma=False
    )
```

time: 585 us -> 190 us (0.32)
  waiting for transfers between devices: 417 us -> 45.1 us
  starting transfers between devices: 0.57 us -> 44.7 us
  local copies, waits for them, and re-layouts: 39.6 us -> 11.3 us
  blocking collectives: 14 us -> 0 us
  between operations: 15.4 us -> 2.52 us
  matrix products: 27.9 us -> 21.3 us
  other arithmetic: 68.5 us -> 62.6 us
    psum x4 -> x0, waiting for transfers between devices: 417 us -> none  [broadcast(): return lax.psum(kept, axis)]
    ppermute x0 -> x8, waiting for transfers between devices: none -> 27.2 us  [the longest x1 17.5 us: on_device(): old_cols = lax.ppermute(old_quarter, ('row', 'col'), swap)]
    all_to_all x0 -> x5, starting transfers between devices: none -> 22.9 us  [the longest x1 5.96 us: on_device(): lax.all_to_all(outgoing, 'row', 0, 0, tiled=True).reshape(row_n, part, -1)]
    ppermute x0 -> x8, starting transfers between devices: none -> 21.8 us  [the longest x1 7.1 us: on_device(): old_cols = lax.ppermute(old_quarter, ('row', 'col'), swap)]
    unnamed x33 -> x23, local copies, waits for them, and re-layouts: 18.7 us -> 0.12 us
    all_to_all x0 -> x5, waiting for transfers between devices: none -> 17.9 us  [the longest x1 16.3 us: on_device(): lax.all_to_all(outgoing, 'col', 0, 0, tiled=True, axis_index_groups=z_gro...]
    all_gather x1 -> x0, blocking collectives: 14 us -> none  [on_device(): gathered = lax.all_gather(masked, 'row', axis=0, tiled=True)]
    another operation x8 -> x5, matrix products: 11.3 us -> 3.11 us  [the longest x3 2.64 us: on_device(): lax.linalg.triangular_solve(lower, eye, left_side=True, lower=True)]
  transfers between devices with their start and end apart: 4 -> 13, of which waited for: 4 -> 8; matrix products, arithmetic and copies ran while one was open for 3% -> 36% of each run, Pallas kernels for 0% -> 0%
where the time goes in v1:
time: 190 us; the launch traced here: 187 us
  other arithmetic  62.6 us (33%)
  waiting for transfers between devices  45.1 us (24%)
  starting transfers between devices  44.7 us (24%)
  matrix products  21.3 us (11%)
  local copies, waits for them, and re-layouts  11.3 us (6%)
  between operations  2.52 us (1%)
    another operation x6, other arithmetic, on_device(): lower = jnp.linalg.cholesky(lead)  34 us
    another operation x3, other arithmetic, on_device(): lax.linalg.triangular_solve(lower, eye, left_side=True, lower=True)  21.1 us
    ppermute x1, waiting for transfers between devices, on_device(): old_cols = lax.ppermute(old_quarter, ('row', 'col'), swap)  17.5 us
    all_to_all x1, waiting for transfers between devices, on_device(): lax.all_to_all(outgoing, 'col', 0, 0, tiled=True, axis_index_groups=z_gro...  16.3 us
    ppermute x1, starting transfers between devices, on_device(): old_cols = lax.ppermute(old_quarter, ('row', 'col'), swap)  7.1 us
    ppermute x1, waiting for transfers between devices, on_device(): swapped = lax.ppermute(own_slice, ('row', 'col'), swap)  6.46 us
    ppermute x3, starting transfers between devices, on_device(): lax.ppermute(old_panel[d * quarter:(d + 1) * quarter], 'col', [(0, d)])  6.4 us
    ppermute x3, starting transfers between devices, on_device(): moved = lax.ppermute(sent, 'col', [(0, d)])  6.38 us
  transfers between devices with their start and end apart: 13, of which 8 were waited for; matrix products, arithmetic and copies ran while one was open for 36% of the time, Pallas kernels for 0%

profile of v1, /device:TPU:7, one launch (start us, length us, event | category | flops | bytes accessed | tf_op | source)
XLA Modules:
  0.0 187.4 jit_solution(17151237909862573058)
XLA Ops:
  6.8 6.0 %all-to-all-start = ((bf16[8,32,1024]{2,1,0:T(8,128)(2,1)}), bf16[8,32,1024]{2,1,0:T(8,128)(2,1)S(1)}, u32[]{:S(2)}, u32[]{:S(2)}) async-start(bf16[8,32,1024]{2,1,0:T(8,128)(2,1)} %bitcast.5), calls=%async_computation | async-start | bytes 1048576 | tf_op jit(solution)/shard_map/row_scatter/all_to_all | solution.py:64
  12.9 3.8 %collective-permute-start = (bf16[512,256]{1,0:T(8,128)(2,1)S(1)}, bf16[512,256]{1,0:T(8,128)(2,1)S(1)}, u32[]{:S(2)}, u32[]{:S(2)}) collective-permute-start(bf16[512,256]{1,0:T(8,128)(2,1)S(1)} %get-tuple-element.23), channel_id=1, source_target_pairs={{0,3},{32,35},{64,67},{96,99},{128,131},{160,163},{192,195},{224,2... | collective-permute-start | bytes 786440 | tf_op jit(solution)/shard_map/y_scatter/ppermute | solution.py:72
  20.6 3.8 %collective-permute-start.3 = (bf16[64,256]{1,0:T(8,128)(2,1)S(1)}, bf16[64,256]{1,0:T(8,128)(2,1)S(1)}, u32[]{:S(2)}, u32[]{:S(2)}) collective-permute-start(bf16[64,256]{1,0:T(8,128)(2,1)S(1)} %pad_maximum_fusion.12), channel_id=1, source_target_pairs={{0,3},{32,35},{64,67},{96,99},{128,131},{160,163},{192,195},{224,2... | collective-permute-start | bytes 98312 | tf_op jit(solution)/shard_map/y_scatter/ppermute | solution.py:76
  27.1 1.8 collective-permute-done.2
  31.2 3.5 %all-to-all-start.1 = ((bf16[8,128,256]{2,1,0:T(8,128)(2,1)}), bf16[8,128,256]{2,1,0:T(8,128)(2,1)S(1)}, u32[]{:S(2)}, u32[]{:S(2)}) async-start(bf16[8,128,256]{2,1,0:T(8,128)(2,1)} %pad_maximum_fusion.1), calls=%async_computation.1 | async-start | bytes 1048576 | tf_op jit(solution)/shard_map/z_scatter/all_to_all | solution.py:86
  35.4 16.3 %all-to-all-done.1 = bf16[8,128,256]{2,1,0:T(8,128)(2,1)S(1)} async-done(((bf16[8,128,256]{2,1,0:T(8,128)(2,1)}), bf16[8,128,256]{2,1,0:T(8,128)(2,1)S(1)}, u32[]{:S(2)}, u32[]{:S(2)}) %all-to-all-start.1) | async-done | bytes 524320 | tf_op jit(solution)/shard_map/z_scatter/all_to_all | solution.py:86
  52.6 5.8 %all-to-all-start.4 = ((bf16[8,160,256]{2,1,0:T(8,128)(2,1)}), bf16[8,160,256]{2,1,0:T(8,128)(2,1)S(1)}, u32[]{:S(2)}, u32[]{:S(2)}) async-start(bf16[8,160,256]{2,1,0:T(8,128)(2,1)} %broadcast_in_dim.42), calls=%async_computation.4 | async-start | bytes 1310720 | tf_op jit(solution)/shard_map/row_gather/all_to_all | solution.py:100
  58.4 1.9 %collective-permute-start.6 = (bf16[32,512]{1,0:T(8,128)(2,1)S(1)}, bf16[32,512]{1,0:T(8,128)(2,1)S(1)}, u32[]{:S(2)}, u32[]{:S(2)}) collective-permute-start(bf16[32,512]{1,0:T(8,128)(2,1)S(1)} %slice_reduce_fusion), channel_id=1, source_target_pairs={{0,0},{1,1},{2,2},{3,3},{4,32},{5,33},{6,34},{7,35},{8,64},{9,65},... | collective-permute-start | bytes 98312 | tf_op jit(solution)/shard_map/swap_samples/ppermute | solution.py:92
  60.8 6.5 %collective-permute-done.6 = bf16[32,512]{1,0:T(8,128)(2,1)S(1)} collective-permute-done((bf16[32,512]{1,0:T(8,128)(2,1)S(1)}, bf16[32,512]{1,0:T(8,128)(2,1)S(1)}, u32[]{:S(2)}, u32[]{:S(2)}) %collective-permute-start.6) | collective-permute-done | bytes 32800 | tf_op jit(solution)/shard_map/swap_samples/ppermute | solution.py:92
  68.4 3.7 %all-to-all-start.2 = ((bf16[8,128,256]{2,1,0:T(8,128)(2,1)}), bf16[8,128,256]{2,1,0:T(8,128)(2,1)S(1)}, u32[]{:S(2)}, u32[]{:S(2)}) async-start(bf16[8,128,256]{2,1,0:T(8,128)(2,1)} %broadcast_in_dim.36), calls=%async_computation.2 | async-start | bytes 1048576 | tf_op jit(solution)/shard_map/z_gather/all_to_all | solution.py:110
  72.8 11.7 %cholesky.50 = f32[128,128]{1,0:T(8,128)S(1)} custom-call(f32[128,128]{1,0:T(8,128)S(1)} %cholesky.118), custom_call_target="Cholesky" | custom-call | tf_op jit(solution)/shard_map/factor/jit(cholesky)/cholesky | solution.py:155
  84.5 9.8 %custom-call.14 = f32[1,128,128]{1,2,0:T(8,128)S(1)} custom-call(f32[1,128,128]{2,1,0:T(8,128)S(1)} %get-tuple-element.38), custom_call_target="InvertDiagBlocksLowerTriangular" | custom-call | tf_op jit(solution)/shard_map/factor/jit(cholesky)/cholesky | solution.py:155
  94.8 11.7 %cholesky.105 = f32[128,128]{1,0:T(8,128)S(1)} custom-call(f32[128,128]{1,0:T(8,128)S(1)} %convolution_subtract_fusion.2), custom_call_target="Cholesky" | custom-call | tf_op jit(solution)/shard_map/factor/jit(cholesky)/cholesky | solution.py:155
  111.8 4.0 %all-to-all-start.3 = ((bf16[4,1024,256]{2,1,0:T(8,128)(2,1)}), bf16[4,1024,256]{2,1,0:T(8,128)(2,1)S(1)}, u32[]{:S(2)}, u32[]{:S(2)}) async-start(bf16[4,1024,256]{2,1,0:T(8,128)(2,1)} %broadcast_in_dim.37), calls=%async_computation.3 | async-start | bytes 4194304 | tf_op jit(solution)/shard_map/y_gather/all_to_all | solution.py:127
  115.8 5.3 %while.1 = (s32[]{:T(128)}, f32[256,256]{1,0:T(8,128)S(1)}, s32[2,2]{1,0:T(2,128)S(1)}, f32[2,128,128]{2,1,0:T(8,128)}, s32[]{:T(128)}) while((s32[]{:T(128)}, f32[256,256]{1,0:T(8,128)S(1)}, s32[2,2]{1,0:T(2,128)S(1)}, f32[2,128,128]{2,1,0:T(8,128)}, s32[]{:T(128)}) %tuple.38), condition=%wide.while_cond, body=%wide.while_body.sunk | while | flops 2 | bytes 132205 | solution.py:156
  116.4 2.0 %bitcast_dynamic-update-slice_fusion.2 = f32[2,128,128]{2,1,0:T(8,128)} fusion(f32[2,128,128]{2,1,0:T(8,128)} %get-tuple-element.84, s32[]{:T(128)S(6)} %copy.29, f32[256,256]{1,0:T(8,128)S(1)} %get-tuple-element.87, s32[]{:T(128)} %bitcast.122, s32[]{:T(128)} %bitcast.123), kind=kLoop, calls=%fused_computation.clone.1 | loop fusion | bytes 132100 | tf_op jit(solution)/shard_map/factor/triangular_solve
  119.1 2.0 %bitcast_dynamic-update-slice_fusion.2 = f32[2,128,128]{2,1,0:T(8,128)} fusion(f32[2,128,128]{2,1,0:T(8,128)} %get-tuple-element.84, s32[]{:T(128)S(6)} %copy.29, f32[256,256]{1,0:T(8,128)S(1)} %get-tuple-element.87, s32[]{:T(128)} %bitcast.122, s32[]{:T(128)} %bitcast.123), kind=kLoop, calls=%fused_computation.clone.1 | loop fusion | bytes 132100 | tf_op jit(solution)/shard_map/factor/triangular_solve
  121.1 21.1 %custom-call.15 = f32[2,128,128]{1,2,0:T(8,128)} custom-call(f32[2,128,128]{2,1,0:T(8,128)} %get-tuple-element.10), custom_call_target="InvertDiagBlocksLowerTriangular" | custom-call | tf_op jit(solution)/shard_map/factor/triangular_solve | solution.py:156
  144.9 7.1 %collective-permute-start.7 = (bf16[512,256]{1,0:T(8,128)(2,1)}, bf16[512,256]{1,0:T(8,128)(2,1)S(1)}, u32[]{:S(2)}, u32[]{:S(2)}) collective-permute-start(bf16[512,256]{1,0:T(8,128)(2,1)} %bitcast.8), channel_id=1, source_target_pairs={{0,0},{1,1},{2,2},{3,3},{4,32},{5,33},{6,34},{7,35},{8,64},{9,65},... | collective-permute-start | bytes 786440 | tf_op jit(solution)/shard_map/swap_panel/ppermute | solution.py:124
  152.5 17.5 %collective-permute-done.7 = bf16[512,256]{1,0:T(8,128)(2,1)S(1)} collective-permute-done((bf16[512,256]{1,0:T(8,128)(2,1)}, bf16[512,256]{1,0:T(8,128)(2,1)S(1)}, u32[]{:S(2)}, u32[]{:S(2)}) %collective-permute-start.7) | collective-permute-done | bytes 262176 | tf_op jit(solution)/shard_map/swap_panel/ppermute | solution.py:124
  171.7 2.7 %fusion.2 = bf16[2048,512]{1,0:T(8,128)(2,1)S(1)} fusion(bf16[2048,512]{1,0:T(8,128)(2,1)} %param.9, bf16[256,2048]{1,0:T(8,128)(2,1)S(1)} %fusion.25, f32[32,512]{1,0:T(8,128)S(1)} %copy-done.4, bf16[256,256]{1,0:T(8,128)(2,1)S(1)} %bitcast.128, bf16[256,256]{1,0:T(8,128)(2,1)S(1)} %bitcast.130), kind=kOutput, calls=%fused_computation.5 | convolution fusion | flops 543686656 | bytes 5570560 | tf_op jit(solution)/shard_map/new_average/dot_general | solution.py:18
  176.1 1.9 %fusion.24 = f32[2048,256]{1,0:T(8,128)S(1)} fusion(f32[2048,256]{1,0:T(8,128)S(1)} %fusion.7, f32[128,256]{1,0:T(8,128)S(1)} %fusion.40, f32[128,256]{1,0:T(8,128)S(1)} %fusion.36), kind=kOutput, calls=%fused_computation.51 | convolution fusion | flops 1610678272 | bytes 4456448 | tf_op jit(solution)/shard_map/panel_rows/dot_general | solution.py:167
  178.1 3.0 %fusion.3 = f32[2048,256]{1,0:T(8,128)} fusion(f32[2048,256]{1,0:T(8,128)S(1)} %fusion.24, f32[256,256]{1,0:T(8,128)S(1)} %fusion.23, bf16[2048,256]{1,0:T(8,128)(2,1)S(1)} %copy-done.2, pred[2048]{0:T(1024)(128)(4,1)S(1)} %broadcast_compare_fusion), kind=kOutput, calls=%fused_computation.8 | convolution fusion | flops 1612185600 | bytes 5507072 | tf_op jit(solution)/shard_map/solved_rows/dot_general | solution.py:183
  181.1 6.3 %select_select_fusion = f32[2048,512]{1,0:T(8,128)} fusion(bf16[2048,512]{1,0:T(8,128)(2,1)S(1)} %fusion.2, f32[2048,256]{1,0:T(8,128)S(1)} %fusion.24, f32[512,256]{1,0:T(8,128)S(1)} %copy-done.3, s32[512]{0:T(512)S(1)} %iota_add_fusion.1, s32[2048]{0:T(1024)S(1)} %iota_add_fusion, pred[2048]{0:T(1024)(128)(4,1)S(1)} %broadcast_compare_fusion, ...), kind=kOutput, calls=%fused_computation.6 | convolution fusion | flops 3230662656 | bytes 8925696 | tf_op jit(solution)/shard_map/trailing/dot_general | solution.py:175
  (102 shorter events, 30.9 us)
Async XLA Ops:
  0.6 4.9 %copy-start = (bf16[256,512]{1,0:T(8,128)(2,1)S(1)}, bf16[256,512]{1,0:T(8,128)(2,1)}, u32[]{:S(2)}) copy-start(bf16[256,512]{1,0:T(8,128)(2,1)} %param.6) | copy-start | bytes 786436
  0.6 5.3 %slice-start = ((bf16[2048,256]{1,0:T(8,128)(2,1)}), bf16[256,256]{1,0:T(8,128)(2,1)S(1)}, s32[]{:S(2)}) async-start(bf16[2048,256]{1,0:T(8,128)(2,1)} %param.11), calls=%async_computation.5 | async-start | bytes 262144 | tf_op jit(solution)/shard_map/row_scatter/slice | solution.py:63
  0.7 2.4 %copy-start.6 = (s32[8]{0:T(128)S(1)}, s32[8]{0:T(128)}, u32[]{:S(2)}) copy-start(s32[8]{0:T(128)} %param.8) | copy-start | bytes 100
  0.7 4.9 %copy-start.5 = (s32[1,96]{1,0:T(1,128)S(1)}, s32[1,96]{1,0:T(1,128)}, u32[]{:S(2)}) copy-start(s32[1,96]{1,0:T(1,128)} %param.7) | copy-start | bytes 1156
  6.8 13.7 %all-to-all-start = ((bf16[8,32,1024]{2,1,0:T(8,128)(2,1)}), bf16[8,32,1024]{2,1,0:T(8,128)(2,1)S(1)}, u32[]{:S(2)}, u32[]{:S(2)}) async-start(bf16[8,32,1024]{2,1,0:T(8,128)(2,1)} %bitcast.5), calls=%async_computation | async-start | bytes 1048576 | tf_op jit(solution)/shard_map/row_scatter/all_to_all | solution.py:64
  12.9 12.9 %collective-permute-start = (bf16[512,256]{1,0:T(8,128)(2,1)S(1)}, bf16[512,256]{1,0:T(8,128)(2,1)S(1)}, u32[]{:S(2)}, u32[]{:S(2)}) collective-permute-start(bf16[512,256]{1,0:T(8,128)(2,1)S(1)} %get-tuple-element.23), channel_id=1, source_target_pairs={{0,3},{32,35},{64,67},{96,99},{128,131},{160,163},{192,195},{224,2... | collective-permute-start | bytes 786440 | tf_op jit(solution)/shard_map/y_scatter/ppermute | solution.py:72
  16.7 10.4 %collective-permute-start.1 = (bf16[512,256]{1,0:T(8,128)(2,1)S(1)}, bf16[512,256]{1,0:T(8,128)(2,1)S(1)}, u32[]{:S(2)}, u32[]{:S(2)}) collective-permute-start(bf16[512,256]{1,0:T(8,128)(2,1)S(1)} %get-tuple-element.22), channel_id=1, source_target_pairs={{0,2},{32,34},{64,66},{96,98},{128,130},{160,162},{192,194},{224,2... | collective-permute-start | bytes 786440 | tf_op jit(solution)/shard_map/y_scatter/ppermute | solution.py:72
  18.0 10.9 %collective-permute-start.2 = (bf16[512,256]{1,0:T(8,128)(2,1)S(1)}, bf16[512,256]{1,0:T(8,128)(2,1)S(1)}, u32[]{:S(2)}, u32[]{:S(2)}) collective-permute-start(bf16[512,256]{1,0:T(8,128)(2,1)S(1)} %get-tuple-element.21), channel_id=1, source_target_pairs={{0,1},{32,33},{64,65},{96,97},{128,129},{160,161},{192,193},{224,2... | collective-permute-start | bytes 786440 | tf_op jit(solution)/shard_map/y_scatter/ppermute | solution.py:72
  20.6 8.3 %collective-permute-start.3 = (bf16[64,256]{1,0:T(8,128)(2,1)S(1)}, bf16[64,256]{1,0:T(8,128)(2,1)S(1)}, u32[]{:S(2)}, u32[]{:S(2)}) collective-permute-start(bf16[64,256]{1,0:T(8,128)(2,1)S(1)} %pad_maximum_fusion.12), channel_id=1, source_target_pairs={{0,3},{32,35},{64,67},{96,99},{128,131},{160,163},{192,195},{224,2... | collective-permute-start | bytes 98312 | tf_op jit(solution)/shard_map/y_scatter/ppermute | solution.py:76
  24.4 5.1 %collective-permute-start.4 = (bf16[64,256]{1,0:T(8,128)(2,1)S(1)}, bf16[64,256]{1,0:T(8,128)(2,1)S(1)}, u32[]{:S(2)}, u32[]{:S(2)}) collective-permute-start(bf16[64,256]{1,0:T(8,128)(2,1)S(1)} %pad_maximum_fusion.12), channel_id=1, source_target_pairs={{0,2},{32,34},{64,66},{96,98},{128,130},{160,162},{192,194},{224,2... | collective-permute-start | bytes 98312 | tf_op jit(solution)/shard_map/y_scatter/ppermute | solution.py:76
  25.8 4.5 %collective-permute-start.5 = (bf16[64,256]{1,0:T(8,128)(2,1)S(1)}, bf16[64,256]{1,0:T(8,128)(2,1)S(1)}, u32[]{:S(2)}, u32[]{:S(2)}) collective-permute-start(bf16[64,256]{1,0:T(8,128)(2,1)S(1)} %pad_maximum_fusion.12), channel_id=1, source_target_pairs={{0,1},{32,33},{64,65},{96,97},{128,129},{160,161},{192,193},{224,2... | collective-permute-start | bytes 98312 | tf_op jit(solution)/shard_map/y_scatter/ppermute | solution.py:76
  31.2 20.5 %all-to-all-start.1 = ((bf16[8,128,256]{2,1,0:T(8,128)(2,1)}), bf16[8,128,256]{2,1,0:T(8,128)(2,1)S(1)}, u32[]{:S(2)}, u32[]{:S(2)}) async-start(bf16[8,128,256]{2,1,0:T(8,128)(2,1)} %pad_maximum_fusion.1), calls=%async_computation.1 | async-start | bytes 1048576 | tf_op jit(solution)/shard_map/z_scatter/all_to_all | solution.py:86
  52.6 15.0 %all-to-all-start.4 = ((bf16[8,160,256]{2,1,0:T(8,128)(2,1)}), bf16[8,160,256]{2,1,0:T(8,128)(2,1)S(1)}, u32[]{:S(2)}, u32[]{:S(2)}) async-start(bf16[8,160,256]{2,1,0:T(8,128)(2,1)} %broadcast_in_dim.42), calls=%async_computation.4 | async-start | bytes 1310720 | tf_op jit(solution)/shard_map/row_gather/all_to_all | solution.py:100
  58.4 8.9 %collective-permute-start.6 = (bf16[32,512]{1,0:T(8,128)(2,1)S(1)}, bf16[32,512]{1,0:T(8,128)(2,1)S(1)}, u32[]{:S(2)}, u32[]{:S(2)}) collective-permute-start(bf16[32,512]{1,0:T(8,128)(2,1)S(1)} %slice_reduce_fusion), channel_id=1, source_target_pairs={{0,0},{1,1},{2,2},{3,3},{4,32},{5,33},{6,34},{7,35},{8,64},{9,65},... | collective-permute-start | bytes 98312 | tf_op jit(solution)/shard_map/swap_samples/ppermute | solution.py:92
  68.4 40.1 %all-to-all-start.2 = ((bf16[8,128,256]{2,1,0:T(8,128)(2,1)}), bf16[8,128,256]{2,1,0:T(8,128)(2,1)S(1)}, u32[]{:S(2)}, u32[]{:S(2)}) async-start(bf16[8,128,256]{2,1,0:T(8,128)(2,1)} %broadcast_in_dim.36), calls=%async_computation.2 | async-start | bytes 1048576 | tf_op jit(solution)/shard_map/z_gather/all_to_all | solution.py:110
  111.8 59.8 %all-to-all-start.3 = ((bf16[4,1024,256]{2,1,0:T(8,128)(2,1)}), bf16[4,1024,256]{2,1,0:T(8,128)(2,1)S(1)}, u32[]{:S(2)}, u32[]{:S(2)}) async-start(bf16[4,1024,256]{2,1,0:T(8,128)(2,1)} %broadcast_in_dim.37), calls=%async_computation.3 | async-start | bytes 4194304 | tf_op jit(solution)/shard_map/y_gather/all_to_all | solution.py:127
  144.9 25.2 %collective-permute-start.7 = (bf16[512,256]{1,0:T(8,128)(2,1)}, bf16[512,256]{1,0:T(8,128)(2,1)S(1)}, u32[]{:S(2)}, u32[]{:S(2)}) collective-permute-start(bf16[512,256]{1,0:T(8,128)(2,1)} %bitcast.8), channel_id=1, source_target_pairs={{0,0},{1,1},{2,2},{3,3},{4,32},{5,33},{6,34},{7,35},{8,64},{9,65},... | collective-permute-start | bytes 786440 | tf_op jit(solution)/shard_map/swap_panel/ppermute | solution.py:124
  152.2 19.4 %copy-start.4 = (f32[32,512]{1,0:T(8,128)S(1)}, f32[32,512]{1,0:T(8,128)}, u32[]{:S(2)}) copy-start(f32[32,512]{1,0:T(8,128)} %param.10) | copy-start | bytes 196612
  174.4 6.7 %copy-start.1 = (bf16[2048,512]{1,0:T(8,128)(2,1)}, bf16[2048,512]{1,0:T(8,128)(2,1)S(1)}, u32[]{:S(2)}) copy-start(bf16[2048,512]{1,0:T(8,128)(2,1)S(1)} %fusion.2) | copy-start | bytes 6291460
  176.1 1.9 %copy-start.2 = (bf16[2048,256]{1,0:T(8,128)(2,1)S(1)}, bf16[2048,256]{1,0:T(8,128)(2,1)}, u32[]{:S(2)}) copy-start(bf16[2048,256]{1,0:T(8,128)(2,1)} %param.11) | copy-start | bytes 3145732
  178.0 3.0 %copy-start.3 = (f32[512,256]{1,0:T(8,128)S(1)}, f32[512,256]{1,0:T(8,128)}, u32[]{:S(2)}) copy-start(f32[512,256]{1,0:T(8,128)} %fusion.15) | copy-start | bytes 1572868
  178.0 3.0 %copy-start.7 = (pred[512]{0:T(512)(128)(4,1)S(1)}, pred[512]{0:T(512)(128)(4,1)}, u32[]{:S(2)}) copy-start(pred[512]{0:T(512)(128)(4,1)} %broadcast_compare_fusion.1) | copy-start | bytes 1540

commit v2 on v0

v2 whole, which is shorter than its diff:
```python
import functools
import jax
import jax.numpy as jnp
from jax import lax
from jax.experimental import pallas as pl
from jax.experimental.pallas import tpu as pltpu
from jax.sharding import PartitionSpec as P

PANEL = 256
SAMPLES = 256
STEP = 64

ema_decay = 0.95
damping = 1.0
update_weight = (1.0 - ema_decay) / SAMPLES
bf16 = jnp.bfloat16
f32 = jnp.float32


def shape(dims, dtype):
    return jax.ShapeDtypeStruct(dims, dtype)


def params(mib=24):
    return pltpu.CompilerParams(vmem_limit_bytes=mib << 20)


def cost(flops, moved):
    return pl.CostEstimate(flops=flops, bytes_accessed=moved, transcendentals=0)


def split(x):
    hi = x.astype(bf16)
    return hi, (x - hi.astype(f32)).astype(bf16)


def dot_nn(a, b):
    return lax.dot_general(a, b, (((1,), (0,)), ((), ())), preferred_element_type=f32)


def dot_nt(a, b):
    return lax.dot_general(a, b, (((1,), (1,)), ((), ())), preferred_element_type=f32)


def dot_tn(a, b):
    return lax.dot_general(a, b, (((0,), (0,)), ((), ())), preferred_element_type=f32)


def three(dot, a, b):
    return dot(a[0], b[0]) + (dot(a[0], b[1]) + dot(a[1], b[0]))


def row_ids(dims):
    return lax.broadcasted_iota(jnp.int32, dims, 0)


def col_ids(dims):
    return lax.broadcasted_iota(jnp.int32, dims, 1)


def old_panel_kernel(quarter, codes_ref, scales_ref, *out_refs):
    rows = codes_ref.shape[0]
    block = rows // scales_ref.shape[0]
    for i, start in enumerate(range(0, rows, block)):
        old = codes_ref[start : start + block, :].astype(f32) * scales_ref[i : i + 1, :]
        out_refs[start // quarter][start % quarter : start % quarter + block, :] = (
            ema_decay * old
        ).astype(bf16)


def old_panel(codes, scales, y_n):
    rows = codes.shape[0]
    quarter = rows // y_n
    return pl.pallas_call(
        functools.partial(old_panel_kernel, quarter),
        grid=(1,),
        in_specs=[
            pl.BlockSpec((rows, PANEL), lambda i: (0, 0)),
            pl.BlockSpec((scales.shape[0], PANEL), lambda i: (0, 0)),
        ],
        out_specs=[pl.BlockSpec((quarter, PANEL), lambda i: (0, 0))] * y_n,
        out_shape=[shape((quarter, PANEL), bf16)] * y_n,
        compiler_params=params(56),
        cost_estimate=cost(rows * PANEL * 2, rows * PANEL * 4),
        name="old_panel",
    )(codes, scales)


def pick_kernel(count_ref, acts_ref, idx_ref, grad_ref, lead_ref, out_ref):
    row = lax.axis_index("row")
    before = jnp.int32(0)
    here = jnp.int32(0)
    for g in range(count_ref.shape[0]):
        before = before + jnp.where(g < row, count_ref[g], 0)
        here = jnp.where(g == row, count_ref[g], here)
    tokens, width = acts_ref.shape
    capacity = idx_ref.shape[1]
    takes_dims = (SAMPLES, capacity)
    slot = col_ids(takes_dims)
    takes = (row_ids(takes_dims) - before == slot) & (slot < here)
    holds = row_ids((tokens, capacity)) == idx_ref[...]
    one = lambda mask: jnp.where(mask, 1.0, 0.0).astype(bf16)
    choice = dot_nt(one(takes), one(holds)).astype(bf16)
    out_ref[:, :width] = dot_nn(choice, acts_ref[...]).astype(bf16)
    out_ref[:, width : width + grad_ref.shape[1]] = grad_ref[...]
    out_ref[:, width + grad_ref.shape[1] :] = lead_ref[...]


def pick(counts, acts, idx, grad, lead):
    tokens, width = acts.shape
    grad_width = grad.shape[1]
    total = width + grad_width + PANEL
    return pl.pallas_call(
        pick_kernel,
        grid=(1,),
        in_specs=[
            pl.BlockSpec(memory_space=pltpu.SMEM),
            pl.BlockSpec(acts.shape, lambda i: (0, 0)),
            pl.BlockSpec(idx.shape, lambda i: (0, 0)),
            pl.BlockSpec((SAMPLES, grad_width), lambda i: (0, 0)),
            pl.BlockSpec((PANEL, PANEL), lambda i: (0, 0)),
        ],
        out_specs=pl.BlockSpec((SAMPLES, total), lambda i: (0, 0)),
        out_shape=shape((SAMPLES, total), bf16),
        compiler_params=params(),
        cost_estimate=cost(2 * SAMPLES * tokens * width, 3 * SAMPLES * total),
        name="pick",
    )(counts, acts, idx, grad, lead)


def eliminate(block):
    tiles = [block[8 * i : 8 * i + 8] for i in range(STEP // 8)]
    sub = row_ids((8, 2 * STEP))
    for j in range(0, STEP, 2):
        t, k = divmod(j, 8)
        c0 = [jnp.broadcast_to(x[:, j : j + 1], x.shape) for x in tiles[t:]]
        c1 = [jnp.broadcast_to(x[:, j + 1 : j + 2], x.shape) for x in tiles[t:]]
        r0, r1 = tiles[t][k : k + 1], tiles[t][k + 1 : k + 2]
        a, b, c = c0[0][k : k + 1], c0[0][k + 1 : k + 2], c1[0][k + 1 : k + 2]
        s0 = lax.rsqrt(a)
        low = b * s0
        u0 = r0 * s0
        s1 = lax.rsqrt(c - low * low)
        u1 = (r1 - low * u0) * s1
        for i in range(t, STEP // 8):
            v0 = c0[i - t] * s0
            v1 = (c1[i - t] - v0 * low) * s1
            new = tiles[i] - v0 * u0 - v1 * u1
            if i == t:
                kept = jnp.where(sub == k + 1, u1, tiles[i])
                new = jnp.where(sub > k + 1, new, jnp.where(sub == k, u0, kept))
            tiles[i] = new
    return jnp.concatenate(tiles, axis=0)


def factor_kernel(x_ref, old_ref, grad_ref, inv_hi_ref, inv_lo_ref, lead_ref, hi_ref, lo_ref, work):
    x = x_ref[...]
    lead = (old_ref[...].astype(f32) + update_weight * dot_tn(x, x)).astype(bf16).astype(f32)
    dims = (PANEL, PANEL)
    eye = jnp.where(row_ids(dims) == col_ids(dims), 1.0, 0.0)
    work[:, :PANEL] = 0.5 * (lead + lead.T) + damping * eye
    work[:, PANEL:] = eye
    small = jnp.where(row_ids((STEP, STEP)) == col_ids((STEP, STEP)), 1.0, 0.0)
    for start in range(0, PANEL, STEP):
        end = start + STEP
        done = eliminate(jnp.concatenate([work[start:end, start:end], small], axis=1))
        rows = three(dot_nn, split(done[:, STEP:]), split(work[start:end, :]))
        work[start:end, :] = rows
        if end < PANEL:
            hi, lo = split(rows)
            down = three(dot_tn, (hi[:, :PANEL], lo[:, :PANEL]), (hi, lo))
            work[end:, :] = work[end:, :] - down[end:, :]
    inv = split(jnp.where(row_ids(dims) >= col_ids(dims), work[:, PANEL:], 0.0))
    inv_hi_ref[...], inv_lo_ref[...] = inv
    leading = dot_nn(inv[0], grad_ref[...]) + dot_nn(inv[1], grad_ref[...])
    lead_ref[...] = leading
    hi_ref[...], lo_ref[...] = split(leading)


def factor(x_lead, old_lead, grad_lead):
    square = shape((PANEL, PANEL), bf16)
    return pl.pallas_call(
        factor_kernel,
        out_shape=(
            square,
            square,
            shape(grad_lead.shape, f32),
            shape(grad_lead.shape, bf16),
            shape(grad_lead.shape, bf16),
        ),
        scratch_shapes=[pltpu.VMEM((PANEL, 2 * PANEL), f32)],
        compiler_params=params(),
        cost_estimate=cost(16_000_000_000, PANEL * PANEL * 20),
        name="factor",
    )(x_lead, old_lead, grad_lead)


def panel_cols_kernel(x_ref, x_lead_ref, old_ref, inv_hi_ref, inv_lo_ref, hi_ref, lo_ref):
    inv = (inv_hi_ref[...], inv_lo_ref[...])
    product = dot_tn(x_ref[...], x_lead_ref[...])
    lead = (old_ref[...].astype(f32) + update_weight * product).astype(bf16).astype(f32)
    first = lax.axis_index("col") * old_ref.shape[0]
    diagonal = row_ids(lead.shape) + first == col_ids(lead.shape)
    lead = lead + jnp.where(diagonal, damping, 0.0)
    hi_ref[...], lo_ref[...] = split(three(dot_nt, split(lead), inv))


def panel_cols(x_cols, x_lead, old_cols, inv):
    out = shape(old_cols.shape, bf16)
    width = old_cols.shape[0]
    return pl.pallas_call(
        panel_cols_kernel,
        out_shape=(out, out),
        compiler_params=params(),
        cost_estimate=cost(8 * width * PANEL * PANEL, width * PANEL * 8),
        name="panel_cols",
    )(x_cols, x_lead, old_cols, *inv)


def rows_kernel(
    width,
    y_n,
    steps,
    quarter_ref,
    part_ref,
    codes_ref,
    scales_ref,
    grad_ref,
    x_cols_ref,
    x_lead_ref,
    inv_hi_ref,
    inv_lo_ref,
    cols_hi_ref,
    cols_lo_ref,
    lead_ref,
    lead_hi_ref,
    lead_lo_ref,
    *refs,
):
    ema_ref, step_ref, solved_ref = refs[-3:]
    half = pl.program_id(0)

    at = quarter_ref[0] * steps + half
    row = lax.axis_index("row")
    col = lax.axis_index("col")
    rows_here = y_n * steps * PANEL
    old = part_ref[pl.ds(pl.multiple_of(half * PANEL, PANEL), PANEL), :]
    x_at = pl.multiple_of((steps + half) * PANEL, PANEL)
    x = part_ref[pl.ds(x_at, SAMPLES), :]
    product = dot_tn(x, x_cols_ref[...])
    blocks = scales_ref.shape[0] // steps
    block = PANEL // blocks
    scale = scales_ref[:blocks, :]
    for i in range(1, steps):
        scale = jnp.where(half == i, scales_ref[i * blocks : (i + 1) * blocks, :], scale)
    pieces = []
    for i in range(blocks):
        piece = codes_ref[i * block : (i + 1) * block, :].astype(f32) * scale[i : i + 1, :]
        pieces.append(
            (
                ema_decay * piece + update_weight * product[i * block : (i + 1) * block, :]
            ).astype(bf16)
        )
    ema = jnp.concatenate(pieces, axis=0)
    ema_ref[...] = ema
    lead = (old.astype(f32) + update_weight * dot_tn(x, x_lead_ref[...])).astype(bf16)
    lead = lead.astype(f32)
    first_row = row * rows_here + at * PANEL
    is_first = first_row == 0
    square = (PANEL, PANEL)
    on_diagonal = (row_ids(square) + first_row) == col_ids(square)
    lead = lead + jnp.where(on_diagonal, damping, 0.0)
    panel = three(dot_nt, split(lead), (inv_hi_ref[...], inv_lo_ref[...]))
    pair = split(panel)
    wide = (PANEL, width)
    diagonal = (row_ids(wide) + first_row) == (col_ids(wide) + col * width)
    full = ema.astype(f32) + jnp.where(diagonal, damping, 0.0)
    step_ref[...] = full - three(dot_nt, pair, (cols_hi_ref[...], cols_lo_ref[...]))
    solved_ref[...] = grad_ref[...].astype(f32) - three(
        dot_nn, pair, (lead_hi_ref[...], lead_lo_ref[...])
    )

    @pl.when(is_first)
    def _():
        step_ref[...] = jnp.zeros(wide, f32)
        solved_ref[...] = lead_ref[...]

    @pl.when(col == 0)
    def _():
        lower = (row_ids(square) + first_row) >= col_ids(square)
        step_ref[:, :PANEL] = jnp.where(lower, panel, 0.0)


def rows(quarter_at, y_n, part, codes, scales, grad, held, before):
    rows_here, width = codes.shape
    grad_width = grad.shape[1]
    steps = rows_here // y_n // PANEL
    whole = lambda a: pl.BlockSpec(a.shape, lambda i, q: (0,) * a.ndim)
    block = lambda w: pl.BlockSpec((PANEL, w), lambda i, q: (q[0] * steps + i, 0))
    held = list(held)
    before = list(before)
    first = 5 + len(held)
    return pl.pallas_call(
        functools.partial(rows_kernel, width, y_n, steps),
        grid_spec=pltpu.PrefetchScalarGridSpec(
            num_scalar_prefetch=1,
            grid=(steps,),
            in_specs=[
                whole(part),
                block(width),
                pl.BlockSpec((scales.shape[0] // y_n, width), lambda i, q: (q[0], 0)),
                block(grad_width),
            ]
            + [whole(a) for a in held]
            + [pl.BlockSpec(memory_space=pl.ANY)] * len(before),
            out_specs=[block(width), block(width), block(grad_width)],
        ),
        out_shape=[
            shape((rows_here, width), bf16),
            shape((rows_here, width), f32),
            shape((rows_here, grad_width), f32),
        ],
        input_output_aliases={first + i: i for i in range(len(before))},
        compiler_params=params(),
        cost_estimate=cost(
            2 * steps * PANEL * PANEL * (width * 4 + PANEL * 7), steps * PANEL * width * 14
        ),
        name="rows",
    )(quarter_at, part, codes, scales, grad, *held, *before)


VMEM = pl.BlockSpec(memory_space=pltpu.VMEM)
ANYWHERE = pl.BlockSpec(memory_space=pl.ANY)


def shuffle(body, name, out_shapes, operands, ties=()):
    count = len(operands)

    def kernel(*refs):
        body(*refs[:count], *refs[count + len(ties) :])

    moved = sum(2 * o.size for o in operands)
    return pl.pallas_call(
        kernel,
        in_specs=[VMEM] * count + [ANYWHERE] * len(ties),
        out_shape=[shape(dims, bf16) for dims in out_shapes],
        compiler_params=params(),
        cost_estimate=cost(moved, 2 * moved),
        name=name,
    )(*operands, *ties)


def choose_y(y_n, own_ref, *refs):
    y = lax.rem(lax.axis_index("col"), y_n)
    value = own_ref[...]
    for d in range(1, y_n):
        value = jnp.where(y == d, refs[d - 1][...], value)
    return value


def old_quarter_kernel(y_n, *refs):
    refs[-1][...] = choose_y(y_n, *refs[:-1])


def unpack_kernel(row_n, width, grad_width, in_ref, own_ref, sent_ref, grad_ref):
    part = in_ref.shape[0] // row_n
    total = in_ref[:part, :width].astype(f32)
    for g in range(1, row_n):
        total = total + in_ref[g * part : (g + 1) * part, :width].astype(f32)
    own = total.astype(bf16)
    own_ref[...] = own
    sent_ref[:part, :] = own[:, :PANEL]
    sent_ref[part:, :] = in_ref[:part, width + grad_width :]
    grad_ref[...] = in_ref[:part, width : width + grad_width]


def row_pack_kernel(slices_ref, grad_ref, own_ref, out_ref):
    part = grad_ref.shape[0]
    for i in range(out_ref.shape[0]):
        out_ref[i, : 2 * part, :] = slices_ref[: 2 * part, :]
        out_ref[i, 2 * part : 3 * part, :] = grad_ref[...]
        for h in range(own_ref.shape[1] // PANEL):
            out_ref[i, (3 + h) * part : (4 + h) * part, :] = own_ref[:, h * PANEL : (h + 1) * PANEL]


def row_unpack_kernel(in_ref, x_lead_ref, old_lead_ref, grad_ref, cols_ref):
    part = SAMPLES // in_ref.shape[0]
    for i in range(in_ref.shape[0]):
        at = slice(i * part, (i + 1) * part)
        x_lead_ref[at, :] = in_ref[i, :part, :]
        old_lead_ref[at, :] = in_ref[i, part : 2 * part, :]
        grad_ref[at, :] = in_ref[i, 2 * part : 3 * part, :]
        for h in range(cols_ref.shape[1] // PANEL):
            cols_ref[at, h * PANEL : (h + 1) * PANEL] = in_ref[i, (3 + h) * part : (4 + h) * part, :]


def z_pack_kernel(y_n, piece, old_ref, x_ref, *refs):
    slices = choose_y(y_n, *refs[:-1])
    out_ref = refs[-1]
    part = x_ref.shape[0]
    halves = x_ref.shape[1] // PANEL
    for i in range(out_ref.shape[0]):
        out_ref[i, :piece, :] = old_ref[:piece, :]
        for h in range(halves):
            at = piece + h * part
            out_ref[i, at : at + part, :] = x_ref[:, h * PANEL : (h + 1) * PANEL]
        out_ref[i, piece + halves * part :, :] = slices


def z_unpack_kernel(piece, part, halves, in_ref, out_ref, old_ref, slices_ref):
    z_n = in_ref.shape[0]
    for i in range(z_n):
        out_ref[i * piece : (i + 1) * piece, :] = in_ref[i, :piece, :]
        old_ref[i * piece : (i + 1) * piece, :] = in_ref[i, :piece, :]
        for h in range(halves):
            at = z_n * piece + (h * z_n + i) * part
            out_ref[at : at + part, :] = in_ref[i, piece + h * part : piece + (h + 1) * part, :]
    slices_ref[...] = in_ref[0, piece + halves * part :, :]


def on_device(acts, sample_idx, sample_count, codes, scales, grad):
    rows_here, width = codes.shape
    grad_width = grad.shape[1]
    row_n = lax.axis_size("row")
    col_n = lax.axis_size("col")
    y_n = col_n // row_n
    z_n = col_n // y_n
    col = lax.axis_index("col")
    y = col % y_n
    z_groups = [[z * y_n + i for z in range(z_n)] for i in range(y_n)]
    swap = [
        (g * col_n + y_n * r + j, r * col_n + y_n * g + j)
        for g in range(row_n)
        for r in range(row_n)
        for j in range(y_n)
    ]

    def turn(d):
        return [(z * y_n + i, z * y_n + (i + d) % y_n) for z in range(z_n) for i in range(y_n)]

    part = SAMPLES // row_n
    quarter = rows_here // y_n
    piece = quarter // z_n
    halves = width // PANEL

    with jax.named_scope("old_panel"):
        old_quarters = old_panel(codes, scales, y_n)
    with jax.named_scope("old_to_y"):
        moved = [lax.ppermute(old_quarters[d], "col", [(0, d)]) for d in range(1, y_n)]
        (old_quarter,) = shuffle(
            functools.partial(old_quarter_kernel, y_n),
            "old_quarter",
            [(quarter, PANEL)],
            [old_quarters[0], *moved],
        )
    with jax.named_scope("row_scatter"):
        outgoing = pick(sample_count, acts, sample_idx, grad, old_quarters[0])
        incoming = lax.all_to_all(outgoing, "row", 0, 0, tiled=True)
        own_slice, sent, grad_slice = shuffle(
            functools.partial(unpack_kernel, row_n, width, grad_width),
            "unpack",
            [(part, width), (2 * part, PANEL), (part, grad_width)],
            [incoming],
            [old_quarter],
        )
    with jax.named_scope("old_to_z"):
        old_pieces = lax.all_to_all(
            old_quarter, "col", 0, 0, tiled=True, axis_index_groups=z_groups
        )
    with jax.named_scope("slices_to_y"):
        moved = [lax.ppermute(sent, "col", [(0, d)]) for d in range(1, y_n)]
    with jax.named_scope("swap_samples"):
        swapped = lax.ppermute(own_slice, ("row", "col"), swap)
    with jax.named_scope("z_gather"):
        (outgoing,) = shuffle(
            functools.partial(z_pack_kernel, y_n, piece),
            "z_pack",
            [(z_n, piece + (halves + 2) * part, PANEL)],
            [old_pieces, swapped, sent, *moved],
        )
        incoming = lax.all_to_all(outgoing, "col", 0, 0, tiled=True, axis_index_groups=z_groups)
        own_part, own_old, slices = shuffle(
            functools.partial(z_unpack_kernel, piece, part, halves),
            "z_unpack",
            [(quarter + halves * SAMPLES, PANEL), (quarter, PANEL), (2 * part, PANEL)],
            [incoming],
        )
    with jax.named_scope("row_gather"):
        (outgoing,) = shuffle(
            row_pack_kernel,
            "row_pack",
            [(row_n, (3 + halves) * part, PANEL)],
            [slices, grad_slice, own_slice],
        )
        incoming = lax.all_to_all(outgoing, "row", 0, 0, tiled=True)
        x_lead, old_lead, grad_lead, x_cols = shuffle(
            row_unpack_kernel,
            "row_unpack",
            [(SAMPLES, PANEL), (PANEL, PANEL), (PANEL, grad_width), (SAMPLES, width)],
            [incoming],
        )
    with jax.named_scope("parts_over_y"):
        parts = [own_part] + [lax.ppermute(own_part, "col", turn(d)) for d in (1, y_n - 1, y_n // 2)]
    with jax.named_scope("swap_panel"):
        old_cols = lax.ppermute(own_old, ("row", "col"), swap)
    with jax.named_scope("factor"):
        *inv, leading, lead_hi, lead_lo = factor(x_lead, old_lead, grad_lead)
    with jax.named_scope("panel_cols"):
        cols_pair = panel_cols(x_cols, x_lead, old_cols, inv)
    with jax.named_scope("rows"):
        held = (x_cols, x_lead, *inv, *cols_pair, leading, lead_hi, lead_lo)
        outs = ()
        for d, received in zip((0, 1, y_n - 1, y_n // 2), parts):
            at = lax.rem(y - d + y_n, y_n).astype(jnp.int32).reshape(1)
            outs = rows(at, y_n, received, codes, scales, grad, held, outs)
    return tuple(outs)


def solution(mesh):
    in_specs = (
        P("row", "col"),
        P("row", None),
        P(),
        P("row", "col"),
        P("row", "col"),
        P("row", "col"),
    )
    out_specs = (P("row", "col"), P("row", "col"), P("row", "col"))
    return jax.shard_map(
        on_device, mesh=mesh, in_specs=in_specs, out_specs=out_specs, check_vma=False
    )
```

time: 585 us -> 124 us (0.21)
  waiting for transfers between devices: 417 us -> 21.3 us
  other arithmetic: 68.5 us -> 0 us
  starting transfers between devices: 0.57 us -> 41.4 us
  local copies, waits for them, and re-layouts: 39.6 us -> 0.99 us
  Pallas kernels: 0 us -> 36.7 us
  matrix products: 27.9 us -> 0 us
  between operations: 15.4 us -> 0.88 us
  blocking collectives: 14 us -> 21.5 us
    psum x4 -> x0, waiting for transfers between devices: 417 us -> none  [broadcast(): return lax.psum(kept, axis)]
    another operation x10 -> x0, other arithmetic: 58.1 us -> none  [the longest x7 36.9 us: on_device(): lead_factor = broadcast(jnp.linalg.cholesky(own_block), 'row', 0)]
    pallas_call x0 -> x14, Pallas kernels: none -> 36.7 us  [the longest x1 15 us: factor(): pl.pallas_call(factor_kernel, out_shape=(square, square, shape(grad_lead....]
    all_to_all x0 -> x1, blocking collectives: none -> 21.5 us  [on_device(): lax.all_to_all(outgoing, 'col', 0, 0, tiled=True, axis_index_groups=z_gro...]
    all_to_all x0 -> x3, starting transfers between devices: none -> 20.9 us  [the longest x2 17.5 us: on_device(): incoming = lax.all_to_all(outgoing, 'row', 0, 0, tiled=True)]
    ppermute x0 -> x11, starting transfers between devices: none -> 20.5 us  [the longest x3 7.57 us: on_device(): moved = [lax.ppermute(sent, 'col', [(0, d)]) for d in range(1, y_n)]]
    unnamed x33 -> x22, local copies, waits for them, and re-layouts: 18.7 us -> 0.99 us
    ppermute x0 -> x11, waiting for transfers between devices: none -> 17.2 us  [the longest x3 7.28 us: on_device(): lax.ppermute(old_quarters[d], 'col', [(0, d)])]
  transfers between devices with their start and end apart: 4 -> 14, of which waited for: 4 -> 5; matrix products, arithmetic and copies ran while one was open for 3% -> 0% of each run, Pallas kernels for 0% -> 23%
where the time goes in v2:
time: 124 us; the launch traced here: 123 us
  starting transfers between devices  41.4 us (33%)
  Pallas kernels  36.7 us (30%)
  blocking collectives  21.5 us (17%)
  waiting for transfers between devices  21.3 us (17%)
    all_to_all x1, blocking collectives, on_device(): lax.all_to_all(outgoing, 'col', 0, 0, tiled=True, axis_index_groups=z_gro...  21.5 us
    all_to_all x2, starting transfers between devices, on_device(): incoming = lax.all_to_all(outgoing, 'row', 0, 0, tiled=True)  17.5 us
    pallas_call x1, Pallas kernels, factor(): pl.pallas_call(factor_kernel, out_shape=(square, square, shape(grad_lead....  15 us
    pallas_call x4, Pallas kernels, rows(): pl.pallas_call(functools.partial(rows_kernel, width, y_n, steps), grid_sp...  14.3 us
    ppermute x3, starting transfers between devices, on_device(): moved = [lax.ppermute(sent, 'col', [(0, d)]) for d in range(1, y_n)]  7.57 us
    ppermute x3, waiting for transfers between devices, on_device(): lax.ppermute(old_quarters[d], 'col', [(0, d)])  7.28 us
    ppermute x1, waiting for transfers between devices, on_device(): swapped = lax.ppermute(own_slice, ('row', 'col'), swap)  6.59 us
    ppermute x3, starting transfers between devices, on_device(): lax.ppermute(old_quarters[d], 'col', [(0, d)])  5.94 us
  transfers between devices with their start and end apart: 14, of which 5 were waited for; matrix products, arithmetic and copies ran while one was open for 0% of the time, Pallas kernels for 23%

profile of v2, /device:TPU:7, one launch (start us, length us, event | category | flops | bytes accessed | tf_op | source)
XLA Modules:
  0.0 122.8 jit_solution(17544807980284807989)
XLA Ops:
  0.7 2.4 %old_panel.1 = (bf16[512,256]{1,0:T(8,128)(2,1)}, bf16[512,256]{1,0:T(8,128)(2,1)}, bf16[512,256]{1,0:T(8,128)(2,1)}, bf16[512,256]{1,0:T(8,128)(2,1)}) custom-call(bf16[2048,512]{1,0:T(8,128)(2,1)} %codes_ref.9, f32[32,512]{1,0:T(8,128)} %scales_ref.9), custom_call_target="tpu_custom_call" | custom-call | flops 1048576 | bytes 2097152 | tf_op jit(solution)/shard_map/old_panel/old_panel/pallas_call | solution.py:74
  4.0 1.7 %pick.1 = bf16[256,1024]{1,0:T(8,128)(2,1)} custom-call(s32[8]{0:T(128)S(1)} %copy-done.6, bf16[256,512]{1,0:T(8,128)(2,1)S(1)} %copy-done.5, s32[1,96]{1,0:T(1,128)S(1)} %copy-done.7, bf16[2048,256]{1,0:T(8,128)(2,1)S(1)} %copy-done.1, bf16[512,256]{1,0:T(8,128)(2,1)S(1)} %copy-done.3), custom_call_target="tpu_custom_call" | custom-call | flops 67108864 | bytes 786432 | tf_op jit(solution)/shard_map/row_scatter/pick/pallas_call | solution.py:113
  5.7 6.0 %all-to-all-start.1 = ((bf16[8,32,1024]{2,1,0:T(8,128)(2,1)}), bf16[8,32,1024]{2,1,0:T(8,128)(2,1)S(1)}, u32[]{:S(2)}, u32[]{:S(2)}) async-start(bf16[8,32,1024]{2,1,0:T(8,128)(2,1)} %bitcast.3), calls=%async_computation.1 | async-start | bytes 1048576 | tf_op jit(solution)/shard_map/row_scatter/all_to_all | solution.py:458
  11.7 2.3 %collective-permute-start = (bf16[512,256]{1,0:T(8,128)(2,1)S(1)}, bf16[512,256]{1,0:T(8,128)(2,1)S(1)}, u32[]{:S(2)}, u32[]{:S(2)}) collective-permute-start(bf16[512,256]{1,0:T(8,128)(2,1)S(1)} %copy-done.10), channel_id=1, source_target_pairs={{0,1},{32,33},{64,65},{96,97},{128,129},{160,161},{192,193},{224,2... | collective-permute-start | bytes 786440 | tf_op jit(solution)/shard_map/old_to_y/ppermute | solution.py:449
  14.0 2.3 %collective-permute-start.1 = (bf16[512,256]{1,0:T(8,128)(2,1)S(1)}, bf16[512,256]{1,0:T(8,128)(2,1)S(1)}, u32[]{:S(2)}, u32[]{:S(2)}) collective-permute-start(bf16[512,256]{1,0:T(8,128)(2,1)S(1)} %copy-done.9), channel_id=1, source_target_pairs={{0,2},{32,34},{64,66},{96,98},{128,130},{160,162},{192,194},{224,2... | collective-permute-start | bytes 786440 | tf_op jit(solution)/shard_map/old_to_y/ppermute | solution.py:449
  16.3 1.3 %collective-permute-start.2 = (bf16[512,256]{1,0:T(8,128)(2,1)S(1)}, bf16[512,256]{1,0:T(8,128)(2,1)S(1)}, u32[]{:S(2)}, u32[]{:S(2)}) collective-permute-start(bf16[512,256]{1,0:T(8,128)(2,1)S(1)} %copy-done.8), channel_id=1, source_target_pairs={{0,3},{32,35},{64,67},{96,99},{128,131},{160,163},{192,195},{224,2... | collective-permute-start | bytes 786440 | tf_op jit(solution)/shard_map/old_to_y/ppermute | solution.py:449
  17.7 1.7 %collective-permute-done.refs_1_ = bf16[512,256]{1,0:T(8,128)(2,1)S(1)} collective-permute-done((bf16[512,256]{1,0:T(8,128)(2,1)S(1)}, bf16[512,256]{1,0:T(8,128)(2,1)S(1)}, u32[]{:S(2)}, u32[]{:S(2)}) %collective-permute-start) | collective-permute-done | bytes 262176 | tf_op jit(solution)/shard_map/old_to_y/ppermute | solution.py:449
  19.3 5.6 %collective-permute-done.1.refs_2_ = bf16[512,256]{1,0:T(8,128)(2,1)S(1)} collective-permute-done((bf16[512,256]{1,0:T(8,128)(2,1)S(1)}, bf16[512,256]{1,0:T(8,128)(2,1)S(1)}, u32[]{:S(2)}, u32[]{:S(2)}) %collective-permute-start.1) | collective-permute-done | bytes 262176 | tf_op jit(solution)/shard_map/old_to_y/ppermute | solution.py:449
  25.7 3.4 %all-to-all-start = ((bf16[8,64,256]{2,1,0:T(8,128)(2,1)}), bf16[8,64,256]{2,1,0:T(8,128)(2,1)S(1)}, u32[]{:S(2)}, u32[]{:S(2)}) async-start(bf16[8,64,256]{2,1,0:T(8,128)(2,1)} %bitcast.1), calls=%async_computation | async-start | bytes 524288 | tf_op jit(solution)/shard_map/old_to_z/all_to_all | solution.py:467
  30.5 5.0 %collective-permute-start.5 = (bf16[64,256]{1,0:T(8,128)(2,1)S(1)}, bf16[64,256]{1,0:T(8,128)(2,1)S(1)}, u32[]{:S(2)}, u32[]{:S(2)}) collective-permute-start(bf16[64,256]{1,0:T(8,128)(2,1)S(1)} %get-tuple-element.38.refs_2_), channel_id=1, source_target_pairs={{0,2},{32,34},{64,66},{96,98},{128,130},{160,162},{192,194},{224,2... | collective-permute-start | bytes 98312 | tf_op jit(solution)/shard_map/slices_to_y/ppermute | solution.py:471
  36.7 1.9 %collective-permute-start.3 = (bf16[32,512]{1,0:T(8,128)(2,1)S(1)}, bf16[32,512]{1,0:T(8,128)(2,1)S(1)}, u32[]{:S(2)}, u32[]{:S(2)}) collective-permute-start(bf16[32,512]{1,0:T(8,128)(2,1)S(1)} %get-tuple-element.37.refs_2_), channel_id=1, source_target_pairs={{0,0},{1,1},{2,2},{3,3},{4,32},{5,33},{6,34},{7,35},{8,64},{9,65},... | collective-permute-start | bytes 98312 | tf_op jit(solution)/shard_map/swap_samples/ppermute | solution.py:473
  38.7 6.6 %collective-permute-done.3.refs_1_ = bf16[32,512]{1,0:T(8,128)(2,1)S(1)} collective-permute-done((bf16[32,512]{1,0:T(8,128)(2,1)S(1)}, bf16[32,512]{1,0:T(8,128)(2,1)S(1)}, u32[]{:S(2)}, u32[]{:S(2)}) %collective-permute-start.3) | collective-permute-done | bytes 32800 | tf_op jit(solution)/shard_map/swap_samples/ppermute | solution.py:473
  45.4 21.5 %all_to_all.32.refs_0_ = bf16[8,192,256]{2,1,0:T(8,128)(2,1)S(1)} all-to-all(bf16[8,192,256]{2,1,0:T(8,128)(2,1)S(1)} %z_pack.1), channel_id=1, replica_groups={{0,4,8,12,16,20,24,28},{1,5,9,13,17,21,25,29},{2,6,10,14,18,22,26,30},{..., dimensions={0} | all-to-all | bytes 1572864 | tf_op jit(solution)/shard_map/z_gather/all_to_all | solution.py:481
  67.8 11.5 %all-to-all-start.3 = ((bf16[8,160,256]{2,1,0:T(8,128)(2,1)}), bf16[8,160,256]{2,1,0:T(8,128)(2,1)S(1)}, u32[]{:S(2)}, u32[]{:S(2)}) async-start(bf16[8,160,256]{2,1,0:T(8,128)(2,1)} %row_pack.1), calls=%async_computation.3 | async-start | bytes 1310720 | tf_op jit(solution)/shard_map/row_gather/all_to_all | solution.py:495
  79.3 2.7 %collective-permute-start.9 = (bf16[1024,256]{1,0:T(8,128)(2,1)S(1)}, bf16[1024,256]{1,0:T(8,128)(2,1)S(1)}, u32[]{:S(2)}, u32[]{:S(2)}) collective-permute-start(bf16[1024,256]{1,0:T(8,128)(2,1)S(1)} %get-tuple-element.39.part_ref), channel_id=1, source_target_pairs={{0,3},{1,0},{2,1},{3,2},{4,7},{5,4},{6,5},{7,6},{8,11},{9,8},{10,9... | collective-permute-start | bytes 1572872 | tf_op jit(solution)/shard_map/parts_over_y/ppermute | solution.py:503
  82.3 2.1 %collective-permute-start.8 = (bf16[512,256]{1,0:T(8,128)(2,1)S(1)}, bf16[512,256]{1,0:T(8,128)(2,1)}, u32[]{:S(2)}, u32[]{:S(2)}) collective-permute-start(bf16[512,256]{1,0:T(8,128)(2,1)S(1)} %get-tuple-element.48), channel_id=1, source_target_pairs={{0,0},{1,1},{2,2},{3,3},{4,32},{5,33},{6,34},{7,35},{8,64},{9,65},... | collective-permute-start | bytes 786440 | tf_op jit(solution)/shard_map/swap_panel/ppermute | solution.py:505
  84.4 4.1 %all-to-all-done.3.refs_0_ = bf16[8,160,256]{2,1,0:T(8,128)(2,1)S(1)} async-done(((bf16[8,160,256]{2,1,0:T(8,128)(2,1)}), bf16[8,160,256]{2,1,0:T(8,128)(2,1)S(1)}, u32[]{:S(2)}, u32[]{:S(2)}) %all-to-all-start.3) | async-done | bytes 655392 | tf_op jit(solution)/shard_map/row_gather/all_to_all | solution.py:495
  88.6 15.0 %factor.1 = (bf16[256,256]{1,0:T(8,128)(2,1)S(1)}, bf16[256,256]{1,0:T(8,128)(2,1)S(1)}, f32[256,256]{1,0:T(8,128)S(1)}, bf16[256,256]{1,0:T(8,128)(2,1)S(1)}, bf16[256,256]{1,0:T(8,128)(2,1)S(1)}) custom-call(bf16[256,256]{1,0:T(8,128)(2,1)S(1)} %get-tuple-element.43.x_ref.x_lead_ref, bf16[256,256]{1,0:T(8,128)(2,1)S(1)} %get-tuple-element.44.old_ref, ...), custom_call_target="tpu_custom_call" | custom-call | flops 16000000000 | bytes 1310720 | tf_op jit(solution)/shard_map/factor/factor/pallas_call | solution.py:182
  103.6 3.4 %collective-permute-done.8.old_ref = bf16[512,256]{1,0:T(8,128)(2,1)} collective-permute-done((bf16[512,256]{1,0:T(8,128)(2,1)S(1)}, bf16[512,256]{1,0:T(8,128)(2,1)}, u32[]{:S(2)}, u32[]{:S(2)}) %collective-permute-start.8) | collective-permute-done | bytes 262176 | tf_op jit(solution)/shard_map/swap_panel/ppermute | solution.py:505
  106.9 1.6 %panel_cols.1 = (bf16[512,256]{1,0:T(8,128)(2,1)S(1)}, bf16[512,256]{1,0:T(8,128)(2,1)S(1)}) custom-call(bf16[256,512]{1,0:T(8,128)(2,1)S(1)} %get-tuple-element.42.x_ref.x_cols_ref, bf16[256,256]{1,0:T(8,128)(2,1)S(1)} %get-tuple-element.43.x_ref.x_lead_ref, bf16[512,256]{1,0:T(8,128)(2,1)} %collective-permute-done.8.old_ref, ...), custom_call_target="tpu_custom_call" | custom-call | flops 268435456 | bytes 1048576 | tf_op jit(solution)/shard_map/panel_cols/panel_cols/pallas_call | solution.py:211
  108.5 3.4 %rows.4 = (bf16[2048,512]{1,0:T(8,128)(2,1)}, f32[2048,512]{1,0:T(8,128)}, f32[2048,256]{1,0:T(8,128)}) custom-call(s32[1]{0:T(128)} %bitcast.7.quarter_ref, bf16[1024,256]{1,0:T(8,128)(2,1)S(1)} %get-tuple-element.39.part_ref, bf16[2048,512]{1,0:T(8,128)(2,1)S(1)} %copy-done, f32[32,512]{1,0:T(8,128)S(1)} %copy-done.2, bf16[2048,256]{1,0:T(8,128)(2,1)S(1)} %copy-done.1, ...), custom_call_target="tpu_custom_call" | custom-call | flops 1006632960 | bytes 3670016 | tf_op jit(solution)/shard_map/rows/rows/pallas_call | solution.py:303
  111.9 4.4 %rows.5 = (bf16[2048,512]{1,0:T(8,128)(2,1)}, f32[2048,512]{1,0:T(8,128)}, f32[2048,256]{1,0:T(8,128)}) custom-call(s32[1]{0:T(128)} %bitcast.6.quarter_ref, bf16[1024,256]{1,0:T(8,128)(2,1)} %collective-permute-done.10.part_ref, bf16[2048,512]{1,0:T(8,128)(2,1)S(1)} %copy-done, ...), custom_call_target="tpu_custom_call", output_to_operand_aliasing={{0}: (14, {}), {1}: (15, {}), {2}: (16, {})} | custom-call | flops 1006632960 | bytes 3670016 | tf_op jit(solution)/shard_map/rows/rows/pallas_call | solution.py:303
  116.2 3.3 %rows.6 = (bf16[2048,512]{1,0:T(8,128)(2,1)}, f32[2048,512]{1,0:T(8,128)}, f32[2048,256]{1,0:T(8,128)}) custom-call(s32[1]{0:T(128)} %bitcast.5.quarter_ref, bf16[1024,256]{1,0:T(8,128)(2,1)S(1)} %collective-permute-done.9.part_ref, bf16[2048,512]{1,0:T(8,128)(2,1)S(1)} %copy-done, ...), custom_call_target="tpu_custom_call", output_to_operand_aliasing={{0}: (14, {}), {1}: (15, {}), {2}: (16, {})} | custom-call | flops 1006632960 | bytes 3670016 | tf_op jit(solution)/shard_map/rows/rows/pallas_call | solution.py:303
  119.5 3.3 %rows.7 = (bf16[2048,512]{1,0:T(8,128)(2,1)}, f32[2048,512]{1,0:T(8,128)}, f32[2048,256]{1,0:T(8,128)}) custom-call(s32[1]{0:T(128)} %bitcast.quarter_ref, bf16[1024,256]{1,0:T(8,128)(2,1)S(1)} %collective-permute-done.7.part_ref, bf16[2048,512]{1,0:T(8,128)(2,1)S(1)} %copy-done, ...), custom_call_target="tpu_custom_call", output_to_operand_aliasing={{0}: (14, {}), {1}: (15, {}), {2}: (16, {})} | custom-call | flops 1006632960 | bytes 3670016 | tf_op jit(solution)/shard_map/rows/rows/pallas_call | solution.py:303
  (41 shorter events, 5.8 us)
Async XLA Ops:
  0.6 2.4 %copy-start.1 = (bf16[2048,256]{1,0:T(8,128)(2,1)S(1)}, bf16[2048,256]{1,0:T(8,128)(2,1)}, u32[]{:S(2)}) copy-start(bf16[2048,256]{1,0:T(8,128)(2,1)} %grad_ref.9) | copy-start | bytes 3145732
  0.6 2.4 %copy-start.5 = (bf16[256,512]{1,0:T(8,128)(2,1)S(1)}, bf16[256,512]{1,0:T(8,128)(2,1)}, u32[]{:S(2)}) copy-start(bf16[256,512]{1,0:T(8,128)(2,1)} %acts_ref.1) | copy-start | bytes 786436
  0.7 2.4 %copy-start.7 = (s32[1,96]{1,0:T(1,128)S(1)}, s32[1,96]{1,0:T(1,128)}, u32[]{:S(2)}) copy-start(s32[1,96]{1,0:T(1,128)} %idx_ref.1) | copy-start | bytes 1156
  0.7 2.4 %copy-start.6 = (s32[8]{0:T(128)S(1)}, s32[8]{0:T(128)}, u32[]{:S(2)}) copy-start(s32[8]{0:T(128)} %count_ref.1) | copy-start | bytes 100
  4.0 7.7 %copy-start.10 = (bf16[512,256]{1,0:T(8,128)(2,1)S(1)}, bf16[512,256]{1,0:T(8,128)(2,1)}, u32[]{:S(2)}) copy-start(bf16[512,256]{1,0:T(8,128)(2,1)} %get-tuple-element.34) | copy-start | bytes 786436
  4.0 10.0 %copy-start.9 = (bf16[512,256]{1,0:T(8,128)(2,1)S(1)}, bf16[512,256]{1,0:T(8,128)(2,1)}, u32[]{:S(2)}) copy-start(bf16[512,256]{1,0:T(8,128)(2,1)} %get-tuple-element.35) | copy-start | bytes 786436
  4.0 12.3 %copy-start.8 = (bf16[512,256]{1,0:T(8,128)(2,1)S(1)}, bf16[512,256]{1,0:T(8,128)(2,1)}, u32[]{:S(2)}) copy-start(bf16[512,256]{1,0:T(8,128)(2,1)} %get-tuple-element.36) | copy-start | bytes 786436
  4.0 20.9 %copy-start.4 = (bf16[512,256]{1,0:T(8,128)(2,1)S(1)}, bf16[512,256]{1,0:T(8,128)(2,1)}, u32[]{:S(2)}) copy-start(bf16[512,256]{1,0:T(8,128)(2,1)} %get-tuple-element.33.refs_0_.lead_ref) | copy-start | bytes 786436
  5.7 20.0 %all-to-all-start.1 = ((bf16[8,32,1024]{2,1,0:T(8,128)(2,1)}), bf16[8,32,1024]{2,1,0:T(8,128)(2,1)S(1)}, u32[]{:S(2)}, u32[]{:S(2)}) async-start(bf16[8,32,1024]{2,1,0:T(8,128)(2,1)} %bitcast.3), calls=%async_computation.1 | async-start | bytes 1048576 | tf_op jit(solution)/shard_map/row_scatter/all_to_all | solution.py:458
  11.7 7.6 %collective-permute-start = (bf16[512,256]{1,0:T(8,128)(2,1)S(1)}, bf16[512,256]{1,0:T(8,128)(2,1)S(1)}, u32[]{:S(2)}, u32[]{:S(2)}) collective-permute-start(bf16[512,256]{1,0:T(8,128)(2,1)S(1)} %copy-done.10), channel_id=1, source_target_pairs={{0,1},{32,33},{64,65},{96,97},{128,129},{160,161},{192,193},{224,2... | collective-permute-start | bytes 786440 | tf_op jit(solution)/shard_map/old_to_y/ppermute | solution.py:449
  14.0 10.9 %collective-permute-start.1 = (bf16[512,256]{1,0:T(8,128)(2,1)S(1)}, bf16[512,256]{1,0:T(8,128)(2,1)S(1)}, u32[]{:S(2)}, u32[]{:S(2)}) collective-permute-start(bf16[512,256]{1,0:T(8,128)(2,1)S(1)} %copy-done.9), channel_id=1, source_target_pairs={{0,2},{32,34},{64,66},{96,98},{128,130},{160,162},{192,194},{224,2... | collective-permute-start | bytes 786440 | tf_op jit(solution)/shard_map/old_to_y/ppermute | solution.py:449
  16.3 8.6 %collective-permute-start.2 = (bf16[512,256]{1,0:T(8,128)(2,1)S(1)}, bf16[512,256]{1,0:T(8,128)(2,1)S(1)}, u32[]{:S(2)}, u32[]{:S(2)}) collective-permute-start(bf16[512,256]{1,0:T(8,128)(2,1)S(1)} %copy-done.8), channel_id=1, source_target_pairs={{0,3},{32,35},{64,67},{96,99},{128,131},{160,163},{192,195},{224,2... | collective-permute-start | bytes 786440 | tf_op jit(solution)/shard_map/old_to_y/ppermute | solution.py:449
  25.7 19.6 %all-to-all-start = ((bf16[8,64,256]{2,1,0:T(8,128)(2,1)}), bf16[8,64,256]{2,1,0:T(8,128)(2,1)S(1)}, u32[]{:S(2)}, u32[]{:S(2)}) async-start(bf16[8,64,256]{2,1,0:T(8,128)(2,1)} %bitcast.1), calls=%async_computation | async-start | bytes 524288 | tf_op jit(solution)/shard_map/old_to_z/all_to_all | solution.py:467
  29.2 9.5 %collective-permute-start.4 = (bf16[64,256]{1,0:T(8,128)(2,1)S(1)}, bf16[64,256]{1,0:T(8,128)(2,1)S(1)}, u32[]{:S(2)}, u32[]{:S(2)}) collective-permute-start(bf16[64,256]{1,0:T(8,128)(2,1)S(1)} %get-tuple-element.38.refs_2_), channel_id=1, source_target_pairs={{0,1},{32,33},{64,65},{96,97},{128,129},{160,161},{192,193},{224,2... | collective-permute-start | bytes 98312 | tf_op jit(solution)/shard_map/slices_to_y/ppermute | solution.py:471
  30.5 8.2 %collective-permute-start.5 = (bf16[64,256]{1,0:T(8,128)(2,1)S(1)}, bf16[64,256]{1,0:T(8,128)(2,1)S(1)}, u32[]{:S(2)}, u32[]{:S(2)}) collective-permute-start(bf16[64,256]{1,0:T(8,128)(2,1)S(1)} %get-tuple-element.38.refs_2_), channel_id=1, source_target_pairs={{0,2},{32,34},{64,66},{96,98},{128,130},{160,162},{192,194},{224,2... | collective-permute-start | bytes 98312 | tf_op jit(solution)/shard_map/slices_to_y/ppermute | solution.py:471
  35.4 3.3 %collective-permute-start.6 = (bf16[64,256]{1,0:T(8,128)(2,1)S(1)}, bf16[64,256]{1,0:T(8,128)(2,1)S(1)}, u32[]{:S(2)}, u32[]{:S(2)}) collective-permute-start(bf16[64,256]{1,0:T(8,128)(2,1)S(1)} %get-tuple-element.38.refs_2_), channel_id=1, source_target_pairs={{0,3},{32,35},{64,67},{96,99},{128,131},{160,163},{192,195},{224,2... | collective-permute-start | bytes 98312 | tf_op jit(solution)/shard_map/slices_to_y/ppermute | solution.py:471
  36.7 8.6 %collective-permute-start.3 = (bf16[32,512]{1,0:T(8,128)(2,1)S(1)}, bf16[32,512]{1,0:T(8,128)(2,1)S(1)}, u32[]{:S(2)}, u32[]{:S(2)}) collective-permute-start(bf16[32,512]{1,0:T(8,128)(2,1)S(1)} %get-tuple-element.37.refs_2_), channel_id=1, source_target_pairs={{0,0},{1,1},{2,2},{3,3},{4,32},{5,33},{6,34},{7,35},{8,64},{9,65},... | collective-permute-start | bytes 98312 | tf_op jit(solution)/shard_map/swap_samples/ppermute | solution.py:473
  67.8 20.7 %all-to-all-start.3 = ((bf16[8,160,256]{2,1,0:T(8,128)(2,1)}), bf16[8,160,256]{2,1,0:T(8,128)(2,1)S(1)}, u32[]{:S(2)}, u32[]{:S(2)}) async-start(bf16[8,160,256]{2,1,0:T(8,128)(2,1)} %row_pack.1), calls=%async_computation.3 | async-start | bytes 1310720 | tf_op jit(solution)/shard_map/row_gather/all_to_all | solution.py:495
  79.3 32.5 %collective-permute-start.10 = (bf16[1024,256]{1,0:T(8,128)(2,1)S(1)}, bf16[1024,256]{1,0:T(8,128)(2,1)}, u32[]{:S(2)}, u32[]{:S(2)}) collective-permute-start(bf16[1024,256]{1,0:T(8,128)(2,1)S(1)} %get-tuple-element.39.part_ref), channel_id=1, source_target_pairs={{0,1},{1,2},{2,3},{3,0},{4,5},{5,6},{6,7},{7,4},{8,9},{9,10},{10,1... | collective-permute-start | bytes 1572872 | tf_op jit(solution)/shard_map/parts_over_y/ppermute | solution.py:503
  79.3 36.9 %collective-permute-start.9 = (bf16[1024,256]{1,0:T(8,128)(2,1)S(1)}, bf16[1024,256]{1,0:T(8,128)(2,1)S(1)}, u32[]{:S(2)}, u32[]{:S(2)}) collective-permute-start(bf16[1024,256]{1,0:T(8,128)(2,1)S(1)} %get-tuple-element.39.part_ref), channel_id=1, source_target_pairs={{0,3},{1,0},{2,1},{3,2},{4,7},{5,4},{6,5},{7,6},{8,11},{9,8},{10,9... | collective-permute-start | bytes 1572872 | tf_op jit(solution)/shard_map/parts_over_y/ppermute | solution.py:503
  82.0 37.5 %collective-permute-start.7 = (bf16[1024,256]{1,0:T(8,128)(2,1)S(1)}, bf16[1024,256]{1,0:T(8,128)(2,1)S(1)}, u32[]{:S(2)}, u32[]{:S(2)}) collective-permute-start(bf16[1024,256]{1,0:T(8,128)(2,1)S(1)} %get-tuple-element.39.part_ref), channel_id=1, source_target_pairs={{0,2},{1,3},{2,0},{3,1},{4,6},{5,7},{6,4},{7,5},{8,10},{9,11},{10,... | collective-permute-start | bytes 1572872 | tf_op jit(solution)/shard_map/parts_over_y/ppermute | solution.py:503
  82.3 24.6 %collective-permute-start.8 = (bf16[512,256]{1,0:T(8,128)(2,1)S(1)}, bf16[512,256]{1,0:T(8,128)(2,1)}, u32[]{:S(2)}, u32[]{:S(2)}) collective-permute-start(bf16[512,256]{1,0:T(8,128)(2,1)S(1)} %get-tuple-element.48), channel_id=1, source_target_pairs={{0,0},{1,1},{2,2},{3,3},{4,32},{5,33},{6,34},{7,35},{8,64},{9,65},... | collective-permute-start | bytes 786440 | tf_op jit(solution)/shard_map/swap_panel/ppermute | solution.py:505
  88.6 19.9 %copy-start = (bf16[2048,512]{1,0:T(8,128)(2,1)S(1)}, bf16[2048,512]{1,0:T(8,128)(2,1)}, u32[]{:S(2)}) copy-start(bf16[2048,512]{1,0:T(8,128)(2,1)} %codes_ref.9) | copy-start | bytes 6291460
  88.6 19.9 %copy-start.2 = (f32[32,512]{1,0:T(8,128)S(1)}, f32[32,512]{1,0:T(8,128)}, u32[]{:S(2)}) copy-start(f32[32,512]{1,0:T(8,128)} %scales_ref.9) | copy-start | bytes 196612
  (1 other events, 1.0 us)

commit v3 on v2

v3 whole, which is shorter than its diff:
```python
import functools
import jax
import jax.numpy as jnp
from jax import lax
from jax.experimental import pallas as pl
from jax.experimental.pallas import tpu as pltpu
from jax.sharding import PartitionSpec as P

PANEL = 256
SAMPLES = 256
STEP = 128

ema_decay = 0.95
damping = 1.0
update_weight = (1.0 - ema_decay) / SAMPLES
bf16 = jnp.bfloat16
f32 = jnp.float32


def shape(dims, dtype):
    return jax.ShapeDtypeStruct(dims, dtype)


def params(mib=24):
    return pltpu.CompilerParams(vmem_limit_bytes=mib << 20)


def cost(flops, moved):
    return pl.CostEstimate(flops=flops, bytes_accessed=moved, transcendentals=0)


def split(x):
    hi = x.astype(bf16)
    return hi, (x - hi.astype(f32)).astype(bf16)


def dot_nn(a, b):
    return lax.dot_general(a, b, (((1,), (0,)), ((), ())), preferred_element_type=f32)


def dot_nt(a, b):
    return lax.dot_general(a, b, (((1,), (1,)), ((), ())), preferred_element_type=f32)


def dot_tn(a, b):
    return lax.dot_general(a, b, (((0,), (0,)), ((), ())), preferred_element_type=f32)


def twice(x, axis):
    return jnp.concatenate([x, x], axis=axis)


def pair(x, axis):
    return jnp.concatenate(split(x), axis=axis)


def three(dot, a, b):
    return dot(a[0], b[0]) + (dot(a[0], b[1]) + dot(a[1], b[0]))


def row_ids(dims):
    return lax.broadcasted_iota(jnp.int32, dims, 0)


def col_ids(dims):
    return lax.broadcasted_iota(jnp.int32, dims, 1)


def old_panel_kernel(quarter, codes_ref, scales_ref, *out_refs):
    rows = codes_ref.shape[0]
    block = rows // scales_ref.shape[0]
    for i, start in enumerate(range(0, rows, block)):
        old = codes_ref[start : start + block, :].astype(f32) * scales_ref[i : i + 1, :]
        out_refs[start // quarter][start % quarter : start % quarter + block, :] = (
            ema_decay * old
        ).astype(bf16)


def old_panel(codes, scales, y_n):
    rows = codes.shape[0]
    quarter = rows // y_n
    return pl.pallas_call(
        functools.partial(old_panel_kernel, quarter),
        grid=(1,),
        in_specs=[
            pl.BlockSpec((rows, PANEL), lambda i: (0, 0)),
            pl.BlockSpec((scales.shape[0], PANEL), lambda i: (0, 0)),
        ],
        out_specs=[pl.BlockSpec((quarter, PANEL), lambda i: (0, 0))] * y_n,
        out_shape=[shape((quarter, PANEL), bf16)] * y_n,
        compiler_params=params(),
        cost_estimate=cost(rows * PANEL * 2, rows * PANEL * 4),
        name="old_panel",
    )(codes, scales)


def pick_kernel(block, count_ref, acts_ref, idx_ref, grad_ref, codes_ref, scales_ref, out_ref):
    row = lax.axis_index("row")
    before = jnp.int32(0)
    here = jnp.int32(0)
    for g in range(count_ref.shape[0]):
        before = before + jnp.where(g < row, count_ref[g], 0)
        here = jnp.where(g == row, count_ref[g], here)
    tokens, width = acts_ref.shape
    capacity = idx_ref.shape[1]
    takes_dims = (SAMPLES, capacity)
    slot = col_ids(takes_dims)
    takes = (row_ids(takes_dims) - before == slot) & (slot < here)
    holds = row_ids((tokens, capacity)) == idx_ref[...]
    one = lambda mask: jnp.where(mask, 1.0, 0.0).astype(bf16)
    choice = dot_nt(one(takes), one(holds)).astype(bf16)
    out_ref[:, :width] = dot_nn(choice, acts_ref[...]).astype(bf16)
    out_ref[:, width : width + grad_ref.shape[1]] = grad_ref[...]
    for i, start in enumerate(range(0, PANEL, block)):
        here = slice(start, start + block)
        old = ema_decay * (codes_ref[here, :].astype(f32) * scales_ref[i : i + 1, :])
        out_ref[here, width + grad_ref.shape[1] :] = old.astype(bf16)


def pick(counts, acts, idx, grad, codes, scales):
    tokens, width = acts.shape
    grad_width = grad.shape[1]
    total = width + grad_width + PANEL
    block = codes.shape[0] // scales.shape[0]
    return pl.pallas_call(
        functools.partial(pick_kernel, block),
        grid=(1,),
        in_specs=[
            pl.BlockSpec(memory_space=pltpu.SMEM),
            pl.BlockSpec(acts.shape, lambda i: (0, 0)),
            pl.BlockSpec(idx.shape, lambda i: (0, 0)),
            pl.BlockSpec((SAMPLES, grad_width), lambda i: (0, 0)),
            pl.BlockSpec((PANEL, PANEL), lambda i: (0, 0)),
            pl.BlockSpec((8, PANEL), lambda i: (0, 0)),
        ],
        out_specs=pl.BlockSpec((SAMPLES, total), lambda i: (0, 0)),
        out_shape=shape((SAMPLES, total), bf16),
        compiler_params=params(56),
        cost_estimate=cost(2 * SAMPLES * tokens * width, 3 * SAMPLES * total),
        name="pick",
    )(counts, acts, idx, grad, codes, scales)


def eliminate(block):
    tiles = [block[8 * i : 8 * i + 8] for i in range(STEP // 8)]
    sub = row_ids((8, 2 * STEP))
    for j in range(0, STEP, 2):
        t, k = divmod(j, 8)
        c0 = [jnp.broadcast_to(x[:, j : j + 1], x.shape) for x in tiles[t:]]
        c1 = [jnp.broadcast_to(x[:, j + 1 : j + 2], x.shape) for x in tiles[t:]]
        r0, r1 = tiles[t][k : k + 1], tiles[t][k + 1 : k + 2]
        a, b, c = c0[0][k : k + 1], c0[0][k + 1 : k + 2], c1[0][k + 1 : k + 2]
        s0 = lax.rsqrt(a)
        low = b * s0
        u0 = r0 * s0
        s1 = lax.rsqrt(c - low * low)
        u1 = (r1 - low * u0) * s1
        for i in range(t, STEP // 8):
            v0 = c0[i - t] * s0
            v1 = (c1[i - t] - v0 * low) * s1
            new = tiles[i] - v0 * u0 - v1 * u1
            if i == t:
                kept = jnp.where(sub == k + 1, u1, tiles[i])
                new = jnp.where(sub > k + 1, new, jnp.where(sub == k, u0, kept))
            tiles[i] = new
    return jnp.concatenate(tiles, axis=0)


def factor_kernel(x_ref, old_ref, grad_ref, inv_ref, inv_t_ref, lead_ref, lead_twice_ref, work):
    x = x_ref[:, x_ref.shape[1] - PANEL :]
    lead = (old_ref[...].astype(f32) + update_weight * dot_tn(x, x)).astype(bf16).astype(f32)
    dims = (PANEL, PANEL)
    eye = jnp.where(row_ids(dims) == col_ids(dims), 1.0, 0.0)
    work[:, :PANEL] = 0.5 * (lead + lead.T) + damping * eye
    work[:, PANEL:] = eye
    small = jnp.where(row_ids((STEP, STEP)) == col_ids((STEP, STEP)), 1.0, 0.0)
    for start in range(0, PANEL, STEP):
        end = start + STEP
        done = eliminate(jnp.concatenate([work[start:end, start:end], small], axis=1))
        rows = three(dot_nn, split(done[:, STEP:]), split(work[start:end, :]))
        work[start:end, :] = rows
        if end < PANEL:
            hi, lo = split(rows)
            down = three(dot_tn, (hi[:, :PANEL], lo[:, :PANEL]), (hi, lo))
            work[end:, :] = work[end:, :] - down[end:, :]
    inverse = jnp.where(row_ids(dims) >= col_ids(dims), work[:, PANEL:], 0.0)
    inv_ref[...] = pair(inverse, 1)
    inv_t_ref[...] = inverse.T
    inv = split(inverse)
    leading = dot_nn(inv[0], grad_ref[...]) + dot_nn(inv[1], grad_ref[...])
    lead_ref[...] = leading
    lead_twice_ref[...] = twice(leading.astype(bf16), 0)


def factor(x_all, old_lead, grad_lead):
    grad_width = grad_lead.shape[1]
    return pl.pallas_call(
        factor_kernel,
        out_shape=(
            shape((PANEL, 2 * PANEL), bf16),
            shape((PANEL, PANEL), f32),
            shape((PANEL, grad_width), f32),
            shape((2 * PANEL, grad_width), bf16),
        ),
        scratch_shapes=[pltpu.VMEM((PANEL, 2 * PANEL), f32)],
        compiler_params=params(),
        cost_estimate=cost(16_000_000_000, PANEL * PANEL * 20),
        name="factor",
    )(x_all, old_lead, grad_lead)


def panel_cols_kernel(x_ref, old_ref, inv_ref, inv_t_ref, out_ref):
    width = old_ref.shape[0]
    product = dot_tn(x_ref[:, :width], x_ref[:, width:])
    lead = (old_ref[...].astype(f32) + update_weight * product).astype(bf16)
    panel = dot_nt(twice(lead, 1), inv_ref[...])
    out_ref[...] = twice(panel.astype(bf16), 1)

    @pl.when(lax.axis_index("col") == 0)
    def _():
        first = panel[:PANEL] + damping * inv_t_ref[...]
        out_ref[:PANEL, :] = twice(first.astype(bf16), 1)


def panel_cols(x_all, old_cols, inv, inv_t):
    width = old_cols.shape[0]
    return pl.pallas_call(
        panel_cols_kernel,
        out_shape=shape((width, 2 * PANEL), bf16),
        compiler_params=params(),
        cost_estimate=cost(8 * width * PANEL * PANEL, width * PANEL * 8),
        name="panel_cols",
    )(x_all, old_cols, inv, inv_t)


def rows_kernel(
    width,
    part_n,
    halves,
    at_ref,
    codes_ref,
    scales_ref,
    grad_ref,
    x_all_ref,
    inv_ref,
    inv_t_ref,
    cols_ref,
    lead_ref,
    lead_twice_ref,
    *refs,
):
    part_refs = refs[:part_n]
    ema_ref, step_ref, solved_ref, part_ref = refs[part_n:]
    at = at_ref[pl.program_id(0)]
    row = lax.axis_index("row")
    col = lax.axis_index("col")
    count = halves * PANEL
    first_row = (row * part_n + at) * count
    for d in range(part_n):

        @pl.when(pl.program_id(0) == d)
        def _():
            part_ref[...] = part_refs[d][...]

    scale = ema_decay * scales_ref[...]
    blocks = scales_ref.shape[0] // halves
    block = PANEL // blocks
    for h in range(halves):
        rows_at = slice(h * PANEL, (h + 1) * PANEL)
        x = part_ref[count + h * SAMPLES : count + (h + 1) * SAMPLES, :]
        product = dot_tn(x, x_all_ref[...])
        lead = (part_ref[rows_at, :].astype(f32) + update_weight * product[:, width:]).astype(bf16)
        panel = dot_nt(twice(lead, 1), inv_ref[...])
        sides = pair(panel, 1)
        below = dot_nt(sides, cols_ref[...])
        for k in range(blocks):
            here = slice(k * block, (k + 1) * block)
            there = slice(h * PANEL + k * block, h * PANEL + (k + 1) * block)
            at_scale = h * blocks + k
            old_ema = codes_ref[there, :].astype(f32) * scale[at_scale : at_scale + 1, :]
            ema = (old_ema + update_weight * product[here, :width]).astype(bf16)
            ema_ref[there, :] = ema
            step_ref[there, :] = ema.astype(f32) - below[here, :]
        remainder = grad_ref[rows_at, :].astype(f32) - dot_nn(sides, lead_twice_ref[...])
        solved_ref[rows_at, :] = remainder

        @pl.when(col == 0)
        def _():
            step_ref[rows_at, :PANEL] = panel

    wide = (count, width)
    apart = first_row - col * width

    @pl.when((apart > -count) & (apart < width) & (col > 0))
    def _():
        diagonal = (row_ids(wide) + apart) == col_ids(wide)
        step_ref[...] += jnp.where(diagonal, damping, 0.0)

    @pl.when((apart > -count) & (apart < width) & (col == 0))
    def _():
        after = (count, width - PANEL)
        diagonal = (row_ids(after) + apart) == col_ids(after) + PANEL
        step_ref[:, PANEL:] += jnp.where(diagonal, damping, 0.0)

    @pl.when(first_row == 0)
    def _():
        square = (PANEL, PANEL)
        first = step_ref[:PANEL, :PANEL] + damping * inv_t_ref[...]
        kept = (row_ids(square) >= col_ids(square)) & (col == 0)
        step_ref[:PANEL, :PANEL] = jnp.where(kept, first, 0.0)
        step_ref[:PANEL, PANEL:] = jnp.zeros((PANEL, width - PANEL), f32)
        solved_ref[:PANEL, :] = lead_ref[...]


def rows(parts_at, parts, codes, scales, grad, held):
    rows_here, width = codes.shape
    grad_width = grad.shape[1]
    part_n = len(parts)
    count = rows_here // part_n
    whole = lambda a: pl.BlockSpec(a.shape, lambda i, q: (0,) * a.ndim)
    block = lambda h, w: pl.BlockSpec((h, w), lambda i, q: (q[i], 0))
    out_specs = [block(count, width), block(count, width), block(count, grad_width)]
    return pl.pallas_call(
        functools.partial(rows_kernel, width, part_n, count // PANEL),
        grid_spec=pltpu.PrefetchScalarGridSpec(
            num_scalar_prefetch=1,
            grid=(part_n,),
            in_specs=[
                block(count, width),
                block(scales.shape[0] // part_n, width),
                block(count, grad_width),
            ]
            + [whole(a) for a in (*held, *parts)],
            out_specs=out_specs,
            scratch_shapes=[pltpu.VMEM(parts[0].shape, bf16)],
        ),
        out_shape=[
            shape((rows_here, width), bf16),
            shape((rows_here, width), f32),
            shape((rows_here, grad_width), f32),
        ],
        compiler_params=params(),
        cost_estimate=cost(2 * rows_here * PANEL * (width * 3 + PANEL * 4), rows_here * width * 14),
        name="rows",
    )(parts_at, codes, scales, grad, *held, *parts)


VMEM = pl.BlockSpec(memory_space=pltpu.VMEM)
ANYWHERE = pl.BlockSpec(memory_space=pl.ANY)


def shuffle(body, name, out_shapes, operands, ties=(), room=0):
    count = len(operands)

    def kernel(*refs):
        body(*refs[:count], *refs[count + len(ties) :])

    moved = sum(2 * o.size for o in operands)
    return pl.pallas_call(
        kernel,
        in_specs=[VMEM] * count + [ANYWHERE] * len(ties),
        out_shape=[shape(dims, bf16) for dims in out_shapes],
        compiler_params=params(),
        cost_estimate=cost(moved + room, 2 * moved),
        name=name,
    )(*operands, *ties)


def choose_y(y_n, own_ref, *refs):
    y = lax.rem(lax.axis_index("col"), y_n)
    value = own_ref[...]
    for d in range(1, y_n):
        value = jnp.where(y == d, refs[d - 1][...], value)
    return value


def old_quarter_kernel(y_n, *refs):
    refs[-1][...] = choose_y(y_n, *refs[:-1])


def unpack_kernel(row_n, width, grad_width, in_ref, own_ref, sent_ref, grad_ref):
    part = in_ref.shape[0] // row_n
    total = in_ref[:part, :width].astype(f32)
    for g in range(1, row_n):
        total = total + in_ref[g * part : (g + 1) * part, :width].astype(f32)
    own = total.astype(bf16)
    own_ref[...] = own
    sent_ref[:part, :] = own[:, :PANEL]
    sent_ref[part:, :] = in_ref[:part, width + grad_width :]
    grad_ref[...] = in_ref[:part, width : width + grad_width]


def row_pack_kernel(slices_ref, old_ref, out_ref):
    rows = slices_ref.shape[0]
    for i in range(out_ref.shape[0]):
        out_ref[i, :rows, :] = slices_ref[...]
        out_ref[i, rows:, :] = old_ref[...]


def row_unpack_kernel(cols_in_ref, lead_in_ref, x_ref, old_lead_ref, grad_ref, old_ref):
    row_n = lead_in_ref.shape[0]
    part = SAMPLES // row_n
    each = cols_in_ref.shape[0] // row_n
    piece = old_ref.shape[0] // row_n
    halves = x_ref.shape[1] // PANEL - 1
    for i in range(row_n):
        at = slice(i * part, (i + 1) * part)
        x_ref[at, halves * PANEL :] = lead_in_ref[i, :part, :]
        old_lead_ref[at, :] = lead_in_ref[i, part : 2 * part, :]
        old_ref[i * piece : (i + 1) * piece, :] = lead_in_ref[i, 2 * part :, :]
        first = i * each
        grad_ref[at, :] = cols_in_ref[first : first + part, :]
        for h in range(halves):
            first = first + part
            x_ref[at, h * PANEL : (h + 1) * PANEL] = cols_in_ref[first : first + part, :]


def z_pack_kernel(y_n, piece, old_ref, x_ref, *refs):
    slices = choose_y(y_n, *refs[:-1])
    out_ref = refs[-1]
    part = x_ref.shape[0]
    halves = x_ref.shape[1] // PANEL
    for i in range(out_ref.shape[0]):
        out_ref[i, :piece, :] = old_ref[:piece, :]
        for h in range(halves):
            at = piece + h * part
            out_ref[i, at : at + part, :] = x_ref[:, h * PANEL : (h + 1) * PANEL]
        out_ref[i, piece + halves * part :, :] = slices


def cols_pack_kernel(grad_ref, own_ref, out_ref):
    part = grad_ref.shape[0]
    out_ref[:part, :] = grad_ref[...]
    for h in range(own_ref.shape[1] // PANEL):
        out_ref[(1 + h) * part : (2 + h) * part, :] = own_ref[:, h * PANEL : (h + 1) * PANEL]


def z_unpack_kernel(piece, part, halves, in_ref, out_ref, slices_ref):
    z_n = in_ref.shape[0]
    for i in range(z_n):
        out_ref[i * piece : (i + 1) * piece, :] = in_ref[i, :piece, :]
        for h in range(halves):
            at = z_n * piece + (h * z_n + i) * part
            out_ref[at : at + part, :] = in_ref[i, piece + h * part : piece + (h + 1) * part, :]
    slices_ref[...] = in_ref[0, piece + halves * part :, :]


def on_device(acts, sample_idx, sample_count, codes, scales, grad):
    rows_here, width = codes.shape
    grad_width = grad.shape[1]
    row_n = lax.axis_size("row")
    col_n = lax.axis_size("col")
    y_n = col_n // row_n
    z_n = col_n // y_n
    col = lax.axis_index("col")
    y = col % y_n
    z_groups = [[z * y_n + i for z in range(z_n)] for i in range(y_n)]
    swap = [
        (g * col_n + y_n * r + j, r * col_n + y_n * g + j)
        for g in range(row_n)
        for r in range(row_n)
        for j in range(y_n)
    ]

    def turn(d):
        return [(z * y_n + i, z * y_n + (i + d) % y_n) for z in range(z_n) for i in range(y_n)]

    part = SAMPLES // row_n
    quarter = rows_here // y_n
    piece = quarter // z_n
    halves = width // PANEL

    with jax.named_scope("old_panel"):
        old_quarters = old_panel(codes, scales, y_n)
    with jax.named_scope("old_to_y"):
        far_first = sorted(range(1, y_n), key=lambda d: -min(d, y_n - d))
        moved = {d: lax.ppermute(old_quarters[d], "col", [(0, d)]) for d in far_first}
        moved = [moved[d] for d in range(1, y_n)]
        (old_quarter,) = shuffle(
            functools.partial(old_quarter_kernel, y_n),
            "old_quarter",
            [(quarter, PANEL)],
            [old_quarters[0], *moved],
            room=0,
        )
    with jax.named_scope("row_scatter"):
        outgoing = pick(sample_count, acts, sample_idx, grad, codes, scales)
        incoming = lax.all_to_all(outgoing, "row", 0, 0, tiled=True)
        own_slice, sent, grad_slice = shuffle(
            functools.partial(unpack_kernel, row_n, width, grad_width),
            "unpack",
            [(part, width), (2 * part, PANEL), (part, grad_width)],
            [incoming],
            [old_quarter],
        )
    with jax.named_scope("old_to_z"):
        old_pieces = lax.all_to_all(
            old_quarter, "col", 0, 0, tiled=True, axis_index_groups=z_groups
        )
    with jax.named_scope("slices_to_y"):
        moved = [lax.ppermute(sent, "col", [(0, d)]) for d in range(1, y_n)]
    with jax.named_scope("swap_samples"):
        swapped = lax.ppermute(own_slice, ("row", "col"), swap)
    with jax.named_scope("z_gather"):
        (outgoing,) = shuffle(
            functools.partial(z_pack_kernel, y_n, piece),
            "z_pack",
            [(z_n, piece + (halves + 2) * part, PANEL)],
            [old_pieces, swapped, sent, *moved],
        )
        incoming = lax.all_to_all(outgoing, "col", 0, 0, tiled=True, axis_index_groups=z_groups)
        swapped_old = lax.ppermute(old_pieces[:piece], ("row", "col"), swap)
        (cols_block,) = shuffle(
            cols_pack_kernel,
            "cols_pack",
            [((1 + halves) * part, PANEL)],
            [grad_slice, own_slice],
            [outgoing],
        )
        cols_incoming = lax.all_gather(cols_block, "row", axis=0, tiled=True)
        own_part, slices = shuffle(
            functools.partial(z_unpack_kernel, piece, part, halves),
            "z_unpack",
            [(quarter + halves * SAMPLES, PANEL), (2 * part, PANEL)],
            [incoming],
            [cols_incoming, swapped_old],
        )
    with jax.named_scope("row_gather"):
        (lead_block,) = shuffle(
            row_pack_kernel, "row_pack", [(row_n, 2 * part + piece, PANEL)], [slices, swapped_old]
        )
        incoming = lax.all_to_all(lead_block, "row", 0, 0, tiled=True)
        x_all, old_lead, grad_lead, old_cols = shuffle(
            row_unpack_kernel,
            "row_unpack",
            [(SAMPLES, width + PANEL), (PANEL, PANEL), (PANEL, grad_width), (width, PANEL)],
            [cols_incoming, incoming],
        )
    with jax.named_scope("parts_over_y"):
        parts = [own_part] + [lax.ppermute(own_part, "col", turn(d)) for d in (1, y_n - 1, y_n // 2)]
    with jax.named_scope("factor"):
        inv, inv_t, leading, lead_twice = factor(x_all, old_lead, grad_lead)
    with jax.named_scope("panel_cols"):
        cols = panel_cols(x_all, old_cols, inv, inv_t)
    with jax.named_scope("rows"):
        shifts = jnp.array([0, 1, y_n - 1, y_n // 2], jnp.int32)
        parts_at = (y + y_n - shifts) % y_n
        held = (x_all, inv, inv_t, cols, leading, lead_twice)
        return tuple(rows(parts_at, parts, codes, scales, grad, held))


def solution(mesh):
    in_specs = (
        P("row", "col"),
        P("row", None),
        P(),
        P("row", "col"),
        P("row", "col"),
        P("row", "col"),
    )
    out_specs = (P("row", "col"), P("row", "col"), P("row", "col"))
    return jax.shard_map(
        on_device, mesh=mesh, in_specs=in_specs, out_specs=out_specs, check_vma=False
    )
```

time: 124 us -> 118 us (0.952)
  starting transfers between devices: 41.4 us -> 52.4 us
  blocking collectives: 21.5 us -> 14.1 us
  Pallas kernels: 36.7 us -> 30.1 us
  waiting for transfers between devices: 21.3 us -> 17.9 us
    all_to_all x1 -> x0, blocking collectives: 21.5 us -> none  [on_device(): lax.all_to_all(outgoing, 'col', 0, 0, tiled=True, axis_index_groups=z_gro...]
    all_gather x0 -> x1, blocking collectives: none -> 14.1 us  [on_device(): cols_incoming = lax.all_gather(cols_block, 'row', axis=0, tiled=True)]
    all_to_all x0 -> x2, starting transfers between devices: none -> 13.1 us  [the longest x1 9.53 us: on_device(): incoming = lax.all_to_all(lead_block, 'row', 0, 0, tiled=True)]
    all_to_all x2 -> x1, starting transfers between devices: 17.5 us -> 5.96 us  [on_device(): incoming = lax.all_to_all(outgoing, 'row', 0, 0, tiled=True)]
    ppermute x1, waiting for transfers between devices: 6.59 us -> 0.01 us  [on_device(): swapped = lax.ppermute(own_slice, ('row', 'col'), swap)]
    pallas_call x7 -> x4, Pallas kernels: 32.5 us -> 27.1 us  [the longest x1 13.7 us: factor(): pl.pallas_call(factor_kernel, out_shape=(shape((PANEL, 2 * PANEL), bf16),...]
    ppermute x3, waiting for transfers between devices: 0.01 us -> 4.88 us  [on_device(): lax.ppermute(own_part, 'col', turn(d))]
    all_to_all x0 -> x2, waiting for transfers between devices: none -> 4.68 us  [the longest x1 3.52 us: on_device(): incoming = lax.all_to_all(lead_block, 'row', 0, 0, tiled=True)]
  transfers between devices with their start and end apart: 14 -> 15, of which waited for: 5 -> 7; matrix products, arithmetic and copies ran while one was open for 0% -> 0% of each run, Pallas kernels for 23% -> 13%
where the time goes in v3:
time: 118 us; the launch traced here: 117 us
  starting transfers between devices  52.4 us (44%)
  Pallas kernels  30.1 us (26%)
  waiting for transfers between devices  17.9 us (15%)
  blocking collectives  14.1 us (12%)
  local copies, waits for them, and re-layouts  1.44 us (1%)
    all_gather x1, blocking collectives, on_device(): cols_incoming = lax.all_gather(cols_block, 'row', axis=0, tiled=True)  14.1 us
    pallas_call x1, Pallas kernels, factor(): pl.pallas_call(factor_kernel, out_shape=(shape((PANEL, 2 * PANEL), bf16),...  13.7 us
    pallas_call x1, Pallas kernels, rows(): pl.pallas_call(functools.partial(rows_kernel, width, part_n, count // PAN...  10.5 us
    all_to_all x1, starting transfers between devices, on_device(): incoming = lax.all_to_all(lead_block, 'row', 0, 0, tiled=True)  9.53 us
    ppermute x3, starting transfers between devices, on_device(): moved = [lax.ppermute(sent, 'col', [(0, d)]) for d in range(1, y_n)]  7.69 us
    ppermute x3, waiting for transfers between devices, on_device(): lax.ppermute(old_quarters[d], 'col', [(0, d)])  7.3 us
    ppermute x1, starting transfers between devices, on_device(): swapped_old = lax.ppermute(old_pieces[:piece], ('row', 'col'), swap)  6.41 us
    all_to_all x1, starting transfers between devices, on_device(): incoming = lax.all_to_all(outgoing, 'row', 0, 0, tiled=True)  5.96 us
  transfers between devices with their start and end apart: 15, of which 7 were waited for; matrix products, arithmetic and copies ran while one was open for 0% of the time, Pallas kernels for 13%

profile of v3, /device:TPU:7, one launch (start us, length us, event | category | flops | bytes accessed | tf_op | source)
XLA Modules:
  0.0 116.7 jit_solution(18323352960757497788)
XLA Ops:
  0.7 2.4 %pick.1 = bf16[256,1024]{1,0:T(8,128)(2,1)} custom-call(s32[8]{0:T(128)} %count_ref.1, bf16[256,512]{1,0:T(8,128)(2,1)} %acts_ref.1, s32[1,96]{1,0:T(1,128)} %idx_ref.1, bf16[2048,256]{1,0:T(8,128)(2,1)} %grad_ref.3, bf16[2048,512]{1,0:T(8,128)(2,1)} %codes_ref.5, f32[32,512]{1,0:T(8,128)} %scales_ref.5), custom_call_target="tpu_custom_call" | custom-call | flops 67108864 | bytes 786432 | tf_op jit(solution)/shard_map/row_scatter/pick/pallas_call | solution.py:125
  3.0 6.0 %all-to-all-start = ((bf16[8,32,1024]{2,1,0:T(8,128)(2,1)}), bf16[8,32,1024]{2,1,0:T(8,128)(2,1)S(1)}, u32[]{:S(2)}, u32[]{:S(2)}) async-start(bf16[8,32,1024]{2,1,0:T(8,128)(2,1)} %bitcast.8), calls=%async_computation | async-start | bytes 1048576 | tf_op jit(solution)/shard_map/row_scatter/all_to_all | solution.py:488
  9.3 2.3 %collective-permute-start = (bf16[512,256]{1,0:T(8,128)(2,1)S(1)}, bf16[512,256]{1,0:T(8,128)(2,1)S(1)}, u32[]{:S(2)}, u32[]{:S(2)}) collective-permute-start(bf16[512,256]{1,0:T(8,128)(2,1)S(1)} %get-tuple-element.21), channel_id=1, source_target_pairs={{0,1},{32,33},{64,65},{96,97},{128,129},{160,161},{192,193},{224,2... | collective-permute-start | bytes 786440 | tf_op jit(solution)/shard_map/old_to_y/ppermute | solution.py:477
  11.6 2.3 %collective-permute-start.1 = (bf16[512,256]{1,0:T(8,128)(2,1)S(1)}, bf16[512,256]{1,0:T(8,128)(2,1)S(1)}, u32[]{:S(2)}, u32[]{:S(2)}) collective-permute-start(bf16[512,256]{1,0:T(8,128)(2,1)S(1)} %get-tuple-element.22), channel_id=1, source_target_pairs={{0,2},{32,34},{64,66},{96,98},{128,130},{160,162},{192,194},{224,2... | collective-permute-start | bytes 786440 | tf_op jit(solution)/shard_map/old_to_y/ppermute | solution.py:477
  13.9 1.3 %collective-permute-start.2 = (bf16[512,256]{1,0:T(8,128)(2,1)S(1)}, bf16[512,256]{1,0:T(8,128)(2,1)S(1)}, u32[]{:S(2)}, u32[]{:S(2)}) collective-permute-start(bf16[512,256]{1,0:T(8,128)(2,1)S(1)} %get-tuple-element.23), channel_id=1, source_target_pairs={{0,3},{32,35},{64,67},{96,99},{128,131},{160,163},{192,195},{224,2... | collective-permute-start | bytes 786440 | tf_op jit(solution)/shard_map/old_to_y/ppermute | solution.py:477
  15.3 1.7 %collective-permute-done.refs_1_ = bf16[512,256]{1,0:T(8,128)(2,1)S(1)} collective-permute-done((bf16[512,256]{1,0:T(8,128)(2,1)S(1)}, bf16[512,256]{1,0:T(8,128)(2,1)S(1)}, u32[]{:S(2)}, u32[]{:S(2)}) %collective-permute-start) | collective-permute-done | bytes 262176 | tf_op jit(solution)/shard_map/old_to_y/ppermute | solution.py:477
  16.9 5.6 %collective-permute-done.1.refs_2_ = bf16[512,256]{1,0:T(8,128)(2,1)S(1)} collective-permute-done((bf16[512,256]{1,0:T(8,128)(2,1)S(1)}, bf16[512,256]{1,0:T(8,128)(2,1)S(1)}, u32[]{:S(2)}, u32[]{:S(2)}) %collective-permute-start.1) | collective-permute-done | bytes 262176 | tf_op jit(solution)/shard_map/old_to_y/ppermute | solution.py:477
  23.3 3.4 %all-to-all-start.1 = ((bf16[8,64,256]{2,1,0:T(8,128)(2,1)}), bf16[8,64,256]{2,1,0:T(8,128)(2,1)S(1)}, u32[]{:S(2)}, u32[]{:S(2)}) async-start(bf16[8,64,256]{2,1,0:T(8,128)(2,1)} %bitcast.2), calls=%async_computation.1 | async-start | bytes 524288 | tf_op jit(solution)/shard_map/old_to_z/all_to_all | solution.py:497
  26.8 5.7 %collective-permute-start.3 = (bf16[32,512]{1,0:T(8,128)(2,1)S(1)}, bf16[32,512]{1,0:T(8,128)(2,1)S(1)}, u32[]{:S(2)}, u32[]{:S(2)}) collective-permute-start(bf16[32,512]{1,0:T(8,128)(2,1)S(1)} %get-tuple-element.25.refs_1_), channel_id=1, source_target_pairs={{0,0},{1,1},{2,2},{3,3},{4,32},{5,33},{6,34},{7,35},{8,64},{9,65},... | collective-permute-start | bytes 98312 | tf_op jit(solution)/shard_map/swap_samples/ppermute | solution.py:503
  33.1 3.8 %collective-permute-start.6 = (bf16[64,256]{1,0:T(8,128)(2,1)S(1)}, bf16[64,256]{1,0:T(8,128)(2,1)S(1)}, u32[]{:S(2)}, u32[]{:S(2)}) collective-permute-start(bf16[64,256]{1,0:T(8,128)(2,1)S(1)} %get-tuple-element.26.refs_2_), channel_id=1, source_target_pairs={{0,3},{32,35},{64,67},{96,99},{128,131},{160,163},{192,195},{224,2... | collective-permute-start | bytes 98312 | tf_op jit(solution)/shard_map/slices_to_y/ppermute | solution.py:501
  36.9 2.5 %collective-permute-start.5 = (bf16[64,256]{1,0:T(8,128)(2,1)S(1)}, bf16[64,256]{1,0:T(8,128)(2,1)S(1)}, u32[]{:S(2)}, u32[]{:S(2)}) collective-permute-start(bf16[64,256]{1,0:T(8,128)(2,1)S(1)} %get-tuple-element.26.refs_2_), channel_id=1, source_target_pairs={{0,2},{32,34},{64,66},{96,98},{128,130},{160,162},{192,194},{224,2... | collective-permute-start | bytes 98312 | tf_op jit(solution)/shard_map/slices_to_y/ppermute | solution.py:501
  39.5 1.3 %collective-permute-start.4 = (bf16[64,256]{1,0:T(8,128)(2,1)S(1)}, bf16[64,256]{1,0:T(8,128)(2,1)S(1)}, u32[]{:S(2)}, u32[]{:S(2)}) collective-permute-start(bf16[64,256]{1,0:T(8,128)(2,1)S(1)} %get-tuple-element.26.refs_2_), channel_id=1, source_target_pairs={{0,1},{32,33},{64,65},{96,97},{128,129},{160,161},{192,193},{224,2... | collective-permute-start | bytes 98312 | tf_op jit(solution)/shard_map/slices_to_y/ppermute | solution.py:501
  42.7 3.5 %all-to-all-start.2 = ((bf16[8,192,256]{2,1,0:T(8,128)(2,1)}), bf16[8,192,256]{2,1,0:T(8,128)(2,1)S(1)}, u32[]{:S(2)}, u32[]{:S(2)}) async-start(bf16[8,192,256]{2,1,0:T(8,128)(2,1)} %z_pack.1.refs_2_), calls=%async_computation.2 | async-start | bytes 1572864 | tf_op jit(solution)/shard_map/z_gather/all_to_all | solution.py:511
  46.3 6.4 %collective-permute-start.7 = (bf16[64,256]{1,0:T(8,128)(2,1)S(1)}, bf16[64,256]{1,0:T(8,128)(2,1)S(1)}, u32[]{:S(2)}, u32[]{:S(2)}) collective-permute-start(bf16[64,256]{1,0:T(8,128)(2,1)S(1)} %slice_bitcast_fusion), channel_id=1, source_target_pairs={{0,0},{1,1},{2,2},{3,3},{4,32},{5,33},{6,34},{7,35},{8,64},{9,65},... | collective-permute-start | bytes 98312 | tf_op jit(solution)/shard_map/z_gather/ppermute | solution.py:512
  52.7 14.1 %all_gather.3.refs_1_.refs_0_ = bf16[768,256]{1,0:T(8,128)(2,1)S(1)} all-gather(bf16[96,256]{1,0:T(8,128)(2,1)S(1)} %cols_pack.1), channel_id=1, replica_groups=mesh['row'=8,'col'=32] {'row'}, dimensions={0}, use_global_device_ids=true | all-gather | bytes 442368 | tf_op jit(solution)/shard_map/z_gather/all_gather | solution.py:520
  66.9 1.2 all-to-all-done.2.refs_0_
  69.7 9.5 %all-to-all-start.3 = ((bf16[8,128,256]{2,1,0:T(8,128)(2,1)}), bf16[8,128,256]{2,1,0:T(8,128)(2,1)S(1)}, u32[]{:S(2)}, u32[]{:S(2)}) async-start(bf16[8,128,256]{2,1,0:T(8,128)(2,1)} %row_pack.1), calls=%async_computation.3 | async-start | bytes 1048576 | tf_op jit(solution)/shard_map/row_gather/all_to_all | solution.py:532
  79.2 2.0 %collective-permute-start.10 = (bf16[1024,256]{1,0:T(8,128)(2,1)}, bf16[1024,256]{1,0:T(8,128)(2,1)S(1)}, u32[]{:S(2)}, u32[]{:S(2)}) collective-permute-start(bf16[1024,256]{1,0:T(8,128)(2,1)} %copy-done.6), channel_id=1, source_target_pairs={{0,2},{1,3},{2,0},{3,1},{4,6},{5,7},{6,4},{7,5},{8,10},{9,11},{10,... | collective-permute-start | bytes 1572872 | tf_op jit(solution)/shard_map/parts_over_y/ppermute | solution.py:540
  81.3 2.2 %collective-permute-start.9 = (bf16[1024,256]{1,0:T(8,128)(2,1)}, bf16[1024,256]{1,0:T(8,128)(2,1)}, u32[]{:S(2)}, u32[]{:S(2)}) collective-permute-start(bf16[1024,256]{1,0:T(8,128)(2,1)} %copy-done.6), channel_id=1, source_target_pairs={{0,3},{1,0},{2,1},{3,2},{4,7},{5,4},{6,5},{7,6},{8,11},{9,8},{10,9... | collective-permute-start | bytes 1572872 | tf_op jit(solution)/shard_map/parts_over_y/ppermute | solution.py:540
  83.5 3.5 %all-to-all-done.3.refs_1_ = bf16[8,128,256]{2,1,0:T(8,128)(2,1)S(1)} async-done(((bf16[8,128,256]{2,1,0:T(8,128)(2,1)}), bf16[8,128,256]{2,1,0:T(8,128)(2,1)S(1)}, u32[]{:S(2)}, u32[]{:S(2)}) %all-to-all-start.3) | async-done | bytes 524320 | tf_op jit(solution)/shard_map/row_gather/all_to_all | solution.py:532
  87.1 13.7 %factor.1 = (bf16[256,512]{1,0:T(8,128)(2,1)S(1)}, f32[256,256]{1,0:T(8,128)S(1)}, f32[256,256]{1,0:T(8,128)S(1)}, bf16[512,256]{1,0:T(8,128)(2,1)S(1)}) custom-call(bf16[256,768]{1,0:T(8,128)(2,1)S(1)} %get-tuple-element.28.x_ref.x_all_ref, bf16[256,256]{1,0:T(8,128)(2,1)S(1)} %get-tuple-element.29.old_ref, bf16[256,256]{1,0:T(8,128)(2,1)S(1)} %get-tuple-element.30.grad_ref), custom_call_target="tpu_custom_call" | custom-call | flops 16000000000 | bytes 1310720 | tf_op jit(solution)/shard_map/factor/factor/pallas_call | solution.py:197
  101.3 3.3 %collective-permute-done.9.refs_2_ = bf16[1024,256]{1,0:T(8,128)(2,1)} collective-permute-done((bf16[1024,256]{1,0:T(8,128)(2,1)}, bf16[1024,256]{1,0:T(8,128)(2,1)}, u32[]{:S(2)}, u32[]{:S(2)}) %collective-permute-start.9) | collective-permute-done | bytes 524320 | tf_op jit(solution)/shard_map/parts_over_y/ppermute | solution.py:540
  104.7 1.5 %collective-permute-done.8.refs_1_ = bf16[1024,256]{1,0:T(8,128)(2,1)} collective-permute-done((bf16[1024,256]{1,0:T(8,128)(2,1)}, bf16[1024,256]{1,0:T(8,128)(2,1)}, u32[]{:S(2)}, u32[]{:S(2)}) %collective-permute-start.8) | collective-permute-done | bytes 524320 | tf_op jit(solution)/shard_map/parts_over_y/ppermute | solution.py:540
  106.2 10.5 %rows.1 = (bf16[2048,512]{1,0:T(8,128)(2,1)}, f32[2048,512]{1,0:T(8,128)}, f32[2048,256]{1,0:T(8,128)}) custom-call(s32[4]{0:T(128)S(1)} %and_select_fusion.at_ref, bf16[2048,512]{1,0:T(8,128)(2,1)S(1)} %copy-done, f32[32,512]{1,0:T(8,128)S(1)} %copy-done.3, bf16[2048,256]{1,0:T(8,128)(2,1)S(1)} %copy-done.1, ...), custom_call_target="tpu_custom_call" | custom-call | flops 2684354560 | bytes 14680064 | tf_op jit(solution)/shard_map/rows/rows/pallas_call | solution.py:323
  (39 shorter events, 5.9 us)
Async XLA Ops:
  0.6 8.4 %copy-start.2 = (f32[32,512]{1,0:T(8,128)S(1)}, f32[32,512]{1,0:T(8,128)}, u32[]{:S(2)}) copy-start(f32[32,512]{1,0:T(8,128)} %scales_ref.5) | copy-start | bytes 196612
  0.6 8.4 %copy-start = (bf16[2048,512]{1,0:T(8,128)(2,1)S(1)}, bf16[2048,512]{1,0:T(8,128)(2,1)}, u32[]{:S(2)}) copy-start(bf16[2048,512]{1,0:T(8,128)(2,1)} %codes_ref.5) | copy-start | bytes 6291460
  3.0 20.3 %all-to-all-start = ((bf16[8,32,1024]{2,1,0:T(8,128)(2,1)}), bf16[8,32,1024]{2,1,0:T(8,128)(2,1)S(1)}, u32[]{:S(2)}, u32[]{:S(2)}) async-start(bf16[8,32,1024]{2,1,0:T(8,128)(2,1)} %bitcast.8), calls=%async_computation | async-start | bytes 1048576 | tf_op jit(solution)/shard_map/row_scatter/all_to_all | solution.py:488
  9.3 7.7 %collective-permute-start = (bf16[512,256]{1,0:T(8,128)(2,1)S(1)}, bf16[512,256]{1,0:T(8,128)(2,1)S(1)}, u32[]{:S(2)}, u32[]{:S(2)}) collective-permute-start(bf16[512,256]{1,0:T(8,128)(2,1)S(1)} %get-tuple-element.21), channel_id=1, source_target_pairs={{0,1},{32,33},{64,65},{96,97},{128,129},{160,161},{192,193},{224,2... | collective-permute-start | bytes 786440 | tf_op jit(solution)/shard_map/old_to_y/ppermute | solution.py:477
  11.6 10.9 %collective-permute-start.1 = (bf16[512,256]{1,0:T(8,128)(2,1)S(1)}, bf16[512,256]{1,0:T(8,128)(2,1)S(1)}, u32[]{:S(2)}, u32[]{:S(2)}) collective-permute-start(bf16[512,256]{1,0:T(8,128)(2,1)S(1)} %get-tuple-element.22), channel_id=1, source_target_pairs={{0,2},{32,34},{64,66},{96,98},{128,130},{160,162},{192,194},{224,2... | collective-permute-start | bytes 786440 | tf_op jit(solution)/shard_map/old_to_y/ppermute | solution.py:477
  13.9 8.6 %collective-permute-start.2 = (bf16[512,256]{1,0:T(8,128)(2,1)S(1)}, bf16[512,256]{1,0:T(8,128)(2,1)S(1)}, u32[]{:S(2)}, u32[]{:S(2)}) collective-permute-start(bf16[512,256]{1,0:T(8,128)(2,1)S(1)} %get-tuple-element.23), channel_id=1, source_target_pairs={{0,3},{32,35},{64,67},{96,99},{128,131},{160,163},{192,195},{224,2... | collective-permute-start | bytes 786440 | tf_op jit(solution)/shard_map/old_to_y/ppermute | solution.py:477
  23.3 18.5 %all-to-all-start.1 = ((bf16[8,64,256]{2,1,0:T(8,128)(2,1)}), bf16[8,64,256]{2,1,0:T(8,128)(2,1)S(1)}, u32[]{:S(2)}, u32[]{:S(2)}) async-start(bf16[8,64,256]{2,1,0:T(8,128)(2,1)} %bitcast.2), calls=%async_computation.1 | async-start | bytes 524288 | tf_op jit(solution)/shard_map/old_to_z/all_to_all | solution.py:497
  26.8 14.0 %collective-permute-start.3 = (bf16[32,512]{1,0:T(8,128)(2,1)S(1)}, bf16[32,512]{1,0:T(8,128)(2,1)S(1)}, u32[]{:S(2)}, u32[]{:S(2)}) collective-permute-start(bf16[32,512]{1,0:T(8,128)(2,1)S(1)} %get-tuple-element.25.refs_1_), channel_id=1, source_target_pairs={{0,0},{1,1},{2,2},{3,3},{4,32},{5,33},{6,34},{7,35},{8,64},{9,65},... | collective-permute-start | bytes 98312 | tf_op jit(solution)/shard_map/swap_samples/ppermute | solution.py:503
  32.4 0.6 copy-start.4
  33.1 19.6 %copy-start.5 = (bf16[32,512]{1,0:T(8,128)(2,1)S(1)}, bf16[32,512]{1,0:T(8,128)(2,1)}, u32[]{:S(2)}) copy-start(bf16[32,512]{1,0:T(8,128)(2,1)} %copy-done.4) | copy-start | bytes 98308
  33.1 7.7 %collective-permute-start.6 = (bf16[64,256]{1,0:T(8,128)(2,1)S(1)}, bf16[64,256]{1,0:T(8,128)(2,1)S(1)}, u32[]{:S(2)}, u32[]{:S(2)}) collective-permute-start(bf16[64,256]{1,0:T(8,128)(2,1)S(1)} %get-tuple-element.26.refs_2_), channel_id=1, source_target_pairs={{0,3},{32,35},{64,67},{96,99},{128,131},{160,163},{192,195},{224,2... | collective-permute-start | bytes 98312 | tf_op jit(solution)/shard_map/slices_to_y/ppermute | solution.py:501
  36.9 3.9 %collective-permute-start.5 = (bf16[64,256]{1,0:T(8,128)(2,1)S(1)}, bf16[64,256]{1,0:T(8,128)(2,1)S(1)}, u32[]{:S(2)}, u32[]{:S(2)}) collective-permute-start(bf16[64,256]{1,0:T(8,128)(2,1)S(1)} %get-tuple-element.26.refs_2_), channel_id=1, source_target_pairs={{0,2},{32,34},{64,66},{96,98},{128,130},{160,162},{192,194},{224,2... | collective-permute-start | bytes 98312 | tf_op jit(solution)/shard_map/slices_to_y/ppermute | solution.py:501
  39.5 2.3 %collective-permute-start.4 = (bf16[64,256]{1,0:T(8,128)(2,1)S(1)}, bf16[64,256]{1,0:T(8,128)(2,1)S(1)}, u32[]{:S(2)}, u32[]{:S(2)}) collective-permute-start(bf16[64,256]{1,0:T(8,128)(2,1)S(1)} %get-tuple-element.26.refs_2_), channel_id=1, source_target_pairs={{0,1},{32,33},{64,65},{96,97},{128,129},{160,161},{192,193},{224,2... | collective-permute-start | bytes 98312 | tf_op jit(solution)/shard_map/slices_to_y/ppermute | solution.py:501
  42.7 25.3 %all-to-all-start.2 = ((bf16[8,192,256]{2,1,0:T(8,128)(2,1)}), bf16[8,192,256]{2,1,0:T(8,128)(2,1)S(1)}, u32[]{:S(2)}, u32[]{:S(2)}) async-start(bf16[8,192,256]{2,1,0:T(8,128)(2,1)} %z_pack.1.refs_2_), calls=%async_computation.2 | async-start | bytes 1572864 | tf_op jit(solution)/shard_map/z_gather/all_to_all | solution.py:511
  46.3 20.6 %collective-permute-start.7 = (bf16[64,256]{1,0:T(8,128)(2,1)S(1)}, bf16[64,256]{1,0:T(8,128)(2,1)S(1)}, u32[]{:S(2)}, u32[]{:S(2)}) collective-permute-start(bf16[64,256]{1,0:T(8,128)(2,1)S(1)} %slice_bitcast_fusion), channel_id=1, source_target_pairs={{0,0},{1,1},{2,2},{3,3},{4,32},{5,33},{6,34},{7,35},{8,64},{9,65},... | collective-permute-start | bytes 98312 | tf_op jit(solution)/shard_map/z_gather/ppermute | solution.py:512
  52.7 26.5 %copy-start.8 = (s32[4]{0:T(128)S(1)}, s32[4]{0:T(128)}, u32[]{:S(2)}) copy-start(s32[4]{0:T(128)} %constant.29) | copy-start | bytes 52
  68.1 0.8 copy-start.6
  69.7 17.3 %all-to-all-start.3 = ((bf16[8,128,256]{2,1,0:T(8,128)(2,1)}), bf16[8,128,256]{2,1,0:T(8,128)(2,1)S(1)}, u32[]{:S(2)}, u32[]{:S(2)}) async-start(bf16[8,128,256]{2,1,0:T(8,128)(2,1)} %row_pack.1), calls=%async_computation.3 | async-start | bytes 1048576 | tf_op jit(solution)/shard_map/row_gather/all_to_all | solution.py:532
  79.2 22.1 %collective-permute-start.10 = (bf16[1024,256]{1,0:T(8,128)(2,1)}, bf16[1024,256]{1,0:T(8,128)(2,1)S(1)}, u32[]{:S(2)}, u32[]{:S(2)}) collective-permute-start(bf16[1024,256]{1,0:T(8,128)(2,1)} %copy-done.6), channel_id=1, source_target_pairs={{0,2},{1,3},{2,0},{3,1},{4,6},{5,7},{6,4},{7,5},{8,10},{9,11},{10,... | collective-permute-start | bytes 1572872 | tf_op jit(solution)/shard_map/parts_over_y/ppermute | solution.py:540
  81.3 23.4 %collective-permute-start.9 = (bf16[1024,256]{1,0:T(8,128)(2,1)}, bf16[1024,256]{1,0:T(8,128)(2,1)}, u32[]{:S(2)}, u32[]{:S(2)}) collective-permute-start(bf16[1024,256]{1,0:T(8,128)(2,1)} %copy-done.6), channel_id=1, source_target_pairs={{0,3},{1,0},{2,1},{3,2},{4,7},{5,4},{6,5},{7,6},{8,11},{9,8},{10,9... | collective-permute-start | bytes 1572872 | tf_op jit(solution)/shard_map/parts_over_y/ppermute | solution.py:540
  83.4 22.8 %collective-permute-start.8 = (bf16[1024,256]{1,0:T(8,128)(2,1)}, bf16[1024,256]{1,0:T(8,128)(2,1)}, u32[]{:S(2)}, u32[]{:S(2)}) collective-permute-start(bf16[1024,256]{1,0:T(8,128)(2,1)} %copy-done.6), channel_id=1, source_target_pairs={{0,1},{1,2},{2,3},{3,0},{4,5},{5,6},{6,7},{7,4},{8,9},{9,10},{10,1... | collective-permute-start | bytes 1572872 | tf_op jit(solution)/shard_map/parts_over_y/ppermute | solution.py:540
  87.0 19.2 %copy-start.1 = (bf16[2048,256]{1,0:T(8,128)(2,1)S(1)}, bf16[2048,256]{1,0:T(8,128)(2,1)}, u32[]{:S(2)}) copy-start(bf16[2048,256]{1,0:T(8,128)(2,1)} %grad_ref.3) | copy-start | bytes 3145732
  87.1 19.2 %copy-start.3 = (f32[32,512]{1,0:T(8,128)S(1)}, f32[32,512]{1,0:T(8,128)}, u32[]{:S(2)}) copy-start(f32[32,512]{1,0:T(8,128)} %scales_ref.5) | copy-start | bytes 196612
  87.1 19.1 %copy-start.7 = (bf16[1024,256]{1,0:T(8,128)(2,1)S(1)}, bf16[1024,256]{1,0:T(8,128)(2,1)}, u32[]{:S(2)}) copy-start(bf16[1024,256]{1,0:T(8,128)(2,1)} %copy-done.6) | copy-start | bytes 1572868

commit v4 on v3

--- a/solution.py
+++ b/solution.py
@@ -184,8 +184,9 @@
             down = three(dot_tn, (hi[:, :PANEL], lo[:, :PANEL]), (hi, lo))
             work[end:, :] = work[end:, :] - down[end:, :]
     inverse = jnp.where(row_ids(dims) >= col_ids(dims), work[:, PANEL:], 0.0)
-    inv_ref[...] = pair(inverse, 1)
-    inv_t_ref[...] = inverse.T
+    inverse_t = inverse.T
+    inv_ref[...] = pair(inverse_t, 0)
+    inv_t_ref[...] = inverse_t
     inv = split(inverse)
     leading = dot_nn(inv[0], grad_ref[...]) + dot_nn(inv[1], grad_ref[...])
     lead_ref[...] = leading
@@ -197,7 +198,7 @@
     return pl.pallas_call(
         factor_kernel,
         out_shape=(
-            shape((PANEL, 2 * PANEL), bf16),
+            shape((2 * PANEL, PANEL), bf16),
             shape((PANEL, PANEL), f32),
             shape((PANEL, grad_width), f32),
             shape((2 * PANEL, grad_width), bf16),
@@ -209,32 +210,34 @@
     )(x_all, old_lead, grad_lead)
 
 
-def panel_cols_kernel(x_ref, old_ref, inv_ref, inv_t_ref, out_ref):
+def panel_cols_kernel(x_ref, old_ref, inv_ref, inv_t_ref, lead_ref, out_ref):
     width = old_ref.shape[0]
     product = dot_tn(x_ref[:, :width], x_ref[:, width:])
     lead = (old_ref[...].astype(f32) + update_weight * product).astype(bf16)
-    panel = dot_nt(twice(lead, 1), inv_ref[...])
-    out_ref[...] = twice(panel.astype(bf16), 1)
+    panel = dot_nn(twice(lead, 1), inv_ref[...])
+    out_ref[:, :width] = twice(panel.T.astype(bf16), 0)
+    out_ref[:, width:] = lead_ref[...]
 
     @pl.when(lax.axis_index("col") == 0)
     def _():
         first = panel[:PANEL] + damping * inv_t_ref[...]
-        out_ref[:PANEL, :] = twice(first.astype(bf16), 1)
-
-
-def panel_cols(x_all, old_cols, inv, inv_t):
+        out_ref[:, :PANEL] = twice(first.T.astype(bf16), 0)
+
+
+def panel_cols(x_all, old_cols, inv, inv_t, lead_twice):
     width = old_cols.shape[0]
     return pl.pallas_call(
         panel_cols_kernel,
-        out_shape=shape((width, 2 * PANEL), bf16),
+        out_shape=shape((2 * PANEL, width + lead_twice.shape[1]), bf16),
         compiler_params=params(),
         cost_estimate=cost(8 * width * PANEL * PANEL, width * PANEL * 8),
         name="panel_cols",
-    )(x_all, old_cols, inv, inv_t)
+    )(x_all, old_cols, inv, inv_t, lead_twice)
 
 
 def rows_kernel(
     width,
+    y_n,
     part_n,
     halves,
     at_ref,
@@ -244,18 +247,17 @@
     x_all_ref,
     inv_ref,
     inv_t_ref,
-    cols_ref,
+    weights_ref,
     lead_ref,
-    lead_twice_ref,
     *refs,
 ):
     part_refs = refs[:part_n]
-    ema_ref, step_ref, solved_ref, part_ref = refs[part_n:]
+    ema_ref, step_ref, solved_ref, part_ref = refs[-4:]
     at = at_ref[pl.program_id(0)]
     row = lax.axis_index("row")
     col = lax.axis_index("col")
     count = halves * PANEL
-    first_row = (row * part_n + at) * count
+    first_row = (row * y_n + at) * count
     for d in range(part_n):
 
         @pl.when(pl.program_id(0) == d)
@@ -268,11 +270,10 @@
     for h in range(halves):
         rows_at = slice(h * PANEL, (h + 1) * PANEL)
         x = part_ref[count + h * SAMPLES : count + (h + 1) * SAMPLES, :]
-        product = dot_tn(x, x_all_ref[...])
+        product = dot_nn(x, x_all_ref[...])
         lead = (part_ref[rows_at, :].astype(f32) + update_weight * product[:, width:]).astype(bf16)
-        panel = dot_nt(twice(lead, 1), inv_ref[...])
-        sides = pair(panel, 1)
-        below = dot_nt(sides, cols_ref[...])
+        panel = dot_nn(twice(lead, 1), inv_ref[...])
+        below = dot_nn(pair(panel, 1), weights_ref[...])
         for k in range(blocks):
             here = slice(k * block, (k + 1) * block)
             there = slice(h * PANEL + k * block, h * PANEL + (k + 1) * block)
@@ -280,9 +281,8 @@
             old_ema = codes_ref[there, :].astype(f32) * scale[at_scale : at_scale + 1, :]
             ema = (old_ema + update_weight * product[here, :width]).astype(bf16)
             ema_ref[there, :] = ema
-            step_ref[there, :] = ema.astype(f32) - below[here, :]
-        remainder = grad_ref[rows_at, :].astype(f32) - dot_nn(sides, lead_twice_ref[...])
-        solved_ref[rows_at, :] = remainder
+            step_ref[there, :] = ema.astype(f32) - below[here, :width]
+        solved_ref[rows_at, :] = grad_ref[rows_at, :].astype(f32) - below[:, width:]
 
         @pl.when(col == 0)
         def _():
@@ -312,25 +312,27 @@
         solved_ref[:PANEL, :] = lead_ref[...]
 
 
-def rows(parts_at, parts, codes, scales, grad, held):
+def rows(parts_at, y_n, parts, codes, scales, grad, held, before):
     rows_here, width = codes.shape
     grad_width = grad.shape[1]
     part_n = len(parts)
-    count = rows_here // part_n
+    count = rows_here // y_n
+    first = 4 + len(held) + part_n
     whole = lambda a: pl.BlockSpec(a.shape, lambda i, q: (0,) * a.ndim)
     block = lambda h, w: pl.BlockSpec((h, w), lambda i, q: (q[i], 0))
     out_specs = [block(count, width), block(count, width), block(count, grad_width)]
     return pl.pallas_call(
-        functools.partial(rows_kernel, width, part_n, count // PANEL),
+        functools.partial(rows_kernel, width, y_n, part_n, count // PANEL),
         grid_spec=pltpu.PrefetchScalarGridSpec(
             num_scalar_prefetch=1,
             grid=(part_n,),
             in_specs=[
                 block(count, width),
-                block(scales.shape[0] // part_n, width),
+                block(scales.shape[0] // y_n, width),
                 block(count, grad_width),
             ]
-            + [whole(a) for a in (*held, *parts)],
+            + [whole(a) for a in (*held, *parts)]
+            + [pl.BlockSpec(memory_space=pl.ANY)] * len(before),
             out_specs=out_specs,
             scratch_shapes=[pltpu.VMEM(parts[0].shape, bf16)],
         ),
@@ -339,10 +341,13 @@
             shape((rows_here, width), f32),
             shape((rows_here, grad_width), f32),
         ],
+        input_output_aliases={first + i: i for i in range(len(before))},
         compiler_params=params(),
-        cost_estimate=cost(2 * rows_here * PANEL * (width * 3 + PANEL * 4), rows_here * width * 14),
+        cost_estimate=cost(
+            2 * part_n * count * PANEL * (width * 3 + PANEL * 4), part_n * count * width * 14
+        ),
         name="rows",
-    )(parts_at, codes, scales, grad, *held, *parts)
+    )(parts_at, codes, scales, grad, *held, *parts, *before)
 
 
 VMEM = pl.BlockSpec(memory_space=pltpu.VMEM)
@@ -439,9 +444,11 @@
     z_n = in_ref.shape[0]
     for i in range(z_n):
         out_ref[i * piece : (i + 1) * piece, :] = in_ref[i, :piece, :]
-        for h in range(halves):
-            at = z_n * piece + (h * z_n + i) * part
-            out_ref[at : at + part, :] = in_ref[i, piece + h * part : piece + (h + 1) * part, :]
+    for h in range(halves):
+        x_at = slice(piece + h * part, piece + (h + 1) * part)
+        x = jnp.concatenate([in_ref[i, x_at, :] for i in range(z_n)], axis=0)
+        at = z_n * piece + h * PANEL
+        out_ref[at : at + PANEL, :] = x.T
     slices_ref[...] = in_ref[0, piece + halves * part :, :]
 
 
@@ -521,7 +528,7 @@
         own_part, slices = shuffle(
             functools.partial(z_unpack_kernel, piece, part, halves),
             "z_unpack",
-            [(quarter + halves * SAMPLES, PANEL), (2 * part, PANEL)],
+            [(quarter + halves * PANEL, PANEL), (2 * part, PANEL)],
             [incoming],
             [cols_incoming, swapped_old],
         )
@@ -541,12 +548,14 @@
     with jax.named_scope("factor"):
         inv, inv_t, leading, lead_twice = factor(x_all, old_lead, grad_lead)
     with jax.named_scope("panel_cols"):
-        cols = panel_cols(x_all, old_cols, inv, inv_t)
+        weights = panel_cols(x_all, old_cols, inv, inv_t, lead_twice)
     with jax.named_scope("rows"):
         shifts = jnp.array([0, 1, y_n - 1, y_n // 2], jnp.int32)
         parts_at = (y + y_n - shifts) % y_n
-        held = (x_all, inv, inv_t, cols, leading, lead_twice)
-        return tuple(rows(parts_at, parts, codes, scales, grad, held))
+        held = (x_all, inv, inv_t, weights, leading)
+        outs = rows(parts_at[:1], y_n, parts[:1], codes, scales, grad, held, ())
+        outs = rows(parts_at[1:], y_n, parts[1:], codes, scales, grad, held, outs)
+        return tuple(outs)
 
 
 def solution(mesh):

time: 118 us -> 117 us (level)
  waiting for transfers between devices: 17.9 us -> 14 us
  Pallas kernels: 30.1 us -> 31.4 us
    ppermute x3, waiting for transfers between devices: 4.88 us -> 1.01 us  [on_device(): lax.ppermute(own_part, 'col', turn(d))]
    pallas_call x3 -> x4, Pallas kernels: 24.8 us -> 26 us  [the longest x1 13.7 us: factor(): pl.pallas_call(factor_kernel, out_shape=(shape((2 * PANEL, PANEL), bf16),...]
  transfers between devices with their start and end apart: 15 -> 15, of which waited for: 7 -> 6; matrix products, arithmetic and copies ran while one was open for 0% -> 0% of each run, Pallas kernels for 13% -> 16%
where the time goes in v4:
time: 117 us; the launch traced here: 115 us
  starting transfers between devices  52.3 us (45%)
  Pallas kernels  31.4 us (27%)
  blocking collectives  14.1 us (12%)
  waiting for transfers between devices  14 us (12%)
  local copies, waits for them, and re-layouts  2.1 us (2%)
    all_gather x1, blocking collectives, on_device(): cols_incoming = lax.all_gather(cols_block, 'row', axis=0, tiled=True)  14.1 us
    pallas_call x1, Pallas kernels, factor(): pl.pallas_call(factor_kernel, out_shape=(shape((2 * PANEL, PANEL), bf16),...  13.7 us
    pallas_call x2, Pallas kernels, rows(): pl.pallas_call(functools.partial(rows_kernel, width, y_n, part_n, count /...  11.5 us
    all_to_all x1, starting transfers between devices, on_device(): incoming = lax.all_to_all(lead_block, 'row', 0, 0, tiled=True)  9.53 us
    ppermute x3, starting transfers between devices, on_device(): moved = [lax.ppermute(sent, 'col', [(0, d)]) for d in range(1, y_n)]  7.69 us
    ppermute x3, waiting for transfers between devices, on_device(): lax.ppermute(old_quarters[d], 'col', [(0, d)])  7.3 us
    ppermute x1, starting transfers between devices, on_device(): swapped_old = lax.ppermute(old_pieces[:piece], ('row', 'col'), swap)  6.41 us
    all_to_all x1, starting transfers between devices, on_device(): incoming = lax.all_to_all(outgoing, 'row', 0, 0, tiled=True)  5.96 us
  transfers between devices with their start and end apart: 15, of which 6 were waited for; matrix products, arithmetic and copies ran while one was open for 0% of the time, Pallas kernels for 16%

profile of v4, /device:TPU:7, one launch (start us, length us, event | category | flops | bytes accessed | tf_op | source)
XLA Modules:
  0.0 114.8 jit_solution(11034733154941035479)
XLA Ops:
  0.7 2.4 %pick.1 = bf16[256,1024]{1,0:T(8,128)(2,1)} custom-call(s32[8]{0:T(128)} %count_ref.1, bf16[256,512]{1,0:T(8,128)(2,1)} %acts_ref.1, s32[1,96]{1,0:T(1,128)} %idx_ref.1, bf16[2048,256]{1,0:T(8,128)(2,1)} %grad_ref.5, bf16[2048,512]{1,0:T(8,128)(2,1)} %codes_ref.7, f32[32,512]{1,0:T(8,128)} %scales_ref.7), custom_call_target="tpu_custom_call" | custom-call | flops 67108864 | bytes 786432 | tf_op jit(solution)/shard_map/row_scatter/pick/pallas_call | solution.py:125
  3.0 6.0 %all-to-all-start = ((bf16[8,32,1024]{2,1,0:T(8,128)(2,1)}), bf16[8,32,1024]{2,1,0:T(8,128)(2,1)S(1)}, u32[]{:S(2)}, u32[]{:S(2)}) async-start(bf16[8,32,1024]{2,1,0:T(8,128)(2,1)} %bitcast.10), calls=%async_computation | async-start | bytes 1048576 | tf_op jit(solution)/shard_map/row_scatter/all_to_all | solution.py:495
  9.3 2.3 %collective-permute-start = (bf16[512,256]{1,0:T(8,128)(2,1)S(1)}, bf16[512,256]{1,0:T(8,128)(2,1)S(1)}, u32[]{:S(2)}, u32[]{:S(2)}) collective-permute-start(bf16[512,256]{1,0:T(8,128)(2,1)S(1)} %get-tuple-element.24), channel_id=1, source_target_pairs={{0,1},{32,33},{64,65},{96,97},{128,129},{160,161},{192,193},{224,2... | collective-permute-start | bytes 786440 | tf_op jit(solution)/shard_map/old_to_y/ppermute | solution.py:484
  11.6 2.3 %collective-permute-start.1 = (bf16[512,256]{1,0:T(8,128)(2,1)S(1)}, bf16[512,256]{1,0:T(8,128)(2,1)S(1)}, u32[]{:S(2)}, u32[]{:S(2)}) collective-permute-start(bf16[512,256]{1,0:T(8,128)(2,1)S(1)} %get-tuple-element.25), channel_id=1, source_target_pairs={{0,2},{32,34},{64,66},{96,98},{128,130},{160,162},{192,194},{224,2... | collective-permute-start | bytes 786440 | tf_op jit(solution)/shard_map/old_to_y/ppermute | solution.py:484
  13.9 1.3 %collective-permute-start.2 = (bf16[512,256]{1,0:T(8,128)(2,1)S(1)}, bf16[512,256]{1,0:T(8,128)(2,1)S(1)}, u32[]{:S(2)}, u32[]{:S(2)}) collective-permute-start(bf16[512,256]{1,0:T(8,128)(2,1)S(1)} %get-tuple-element.26), channel_id=1, source_target_pairs={{0,3},{32,35},{64,67},{96,99},{128,131},{160,163},{192,195},{224,2... | collective-permute-start | bytes 786440 | tf_op jit(solution)/shard_map/old_to_y/ppermute | solution.py:484
  15.3 1.7 %collective-permute-done.refs_1_ = bf16[512,256]{1,0:T(8,128)(2,1)S(1)} collective-permute-done((bf16[512,256]{1,0:T(8,128)(2,1)S(1)}, bf16[512,256]{1,0:T(8,128)(2,1)S(1)}, u32[]{:S(2)}, u32[]{:S(2)}) %collective-permute-start) | collective-permute-done | bytes 262176 | tf_op jit(solution)/shard_map/old_to_y/ppermute | solution.py:484
  16.9 5.6 %collective-permute-done.1.refs_2_ = bf16[512,256]{1,0:T(8,128)(2,1)S(1)} collective-permute-done((bf16[512,256]{1,0:T(8,128)(2,1)S(1)}, bf16[512,256]{1,0:T(8,128)(2,1)S(1)}, u32[]{:S(2)}, u32[]{:S(2)}) %collective-permute-start.1) | collective-permute-done | bytes 262176 | tf_op jit(solution)/shard_map/old_to_y/ppermute | solution.py:484
  23.3 3.4 %all-to-all-start.1 = ((bf16[8,64,256]{2,1,0:T(8,128)(2,1)}), bf16[8,64,256]{2,1,0:T(8,128)(2,1)S(1)}, u32[]{:S(2)}, u32[]{:S(2)}) async-start(bf16[8,64,256]{2,1,0:T(8,128)(2,1)} %bitcast.2), calls=%async_computation.1 | async-start | bytes 524288 | tf_op jit(solution)/shard_map/old_to_z/all_to_all | solution.py:504
  26.8 5.7 %collective-permute-start.3 = (bf16[32,512]{1,0:T(8,128)(2,1)S(1)}, bf16[32,512]{1,0:T(8,128)(2,1)S(1)}, u32[]{:S(2)}, u32[]{:S(2)}) collective-permute-start(bf16[32,512]{1,0:T(8,128)(2,1)S(1)} %get-tuple-element.28.refs_1_), channel_id=1, source_target_pairs={{0,0},{1,1},{2,2},{3,3},{4,32},{5,33},{6,34},{7,35},{8,64},{9,65},... | collective-permute-start | bytes 98312 | tf_op jit(solution)/shard_map/swap_samples/ppermute | solution.py:510
  33.1 3.8 %collective-permute-start.6 = (bf16[64,256]{1,0:T(8,128)(2,1)S(1)}, bf16[64,256]{1,0:T(8,128)(2,1)S(1)}, u32[]{:S(2)}, u32[]{:S(2)}) collective-permute-start(bf16[64,256]{1,0:T(8,128)(2,1)S(1)} %get-tuple-element.29.refs_2_), channel_id=1, source_target_pairs={{0,3},{32,35},{64,67},{96,99},{128,131},{160,163},{192,195},{224,2... | collective-permute-start | bytes 98312 | tf_op jit(solution)/shard_map/slices_to_y/ppermute | solution.py:508
  36.9 2.5 %collective-permute-start.5 = (bf16[64,256]{1,0:T(8,128)(2,1)S(1)}, bf16[64,256]{1,0:T(8,128)(2,1)S(1)}, u32[]{:S(2)}, u32[]{:S(2)}) collective-permute-start(bf16[64,256]{1,0:T(8,128)(2,1)S(1)} %get-tuple-element.29.refs_2_), channel_id=1, source_target_pairs={{0,2},{32,34},{64,66},{96,98},{128,130},{160,162},{192,194},{224,2... | collective-permute-start | bytes 98312 | tf_op jit(solution)/shard_map/slices_to_y/ppermute | solution.py:508
  39.5 1.3 %collective-permute-start.4 = (bf16[64,256]{1,0:T(8,128)(2,1)S(1)}, bf16[64,256]{1,0:T(8,128)(2,1)S(1)}, u32[]{:S(2)}, u32[]{:S(2)}) collective-permute-start(bf16[64,256]{1,0:T(8,128)(2,1)S(1)} %get-tuple-element.29.refs_2_), channel_id=1, source_target_pairs={{0,1},{32,33},{64,65},{96,97},{128,129},{160,161},{192,193},{224,2... | collective-permute-start | bytes 98312 | tf_op jit(solution)/shard_map/slices_to_y/ppermute | solution.py:508
  42.7 3.5 %all-to-all-start.2 = ((bf16[8,192,256]{2,1,0:T(8,128)(2,1)}), bf16[8,192,256]{2,1,0:T(8,128)(2,1)S(1)}, u32[]{:S(2)}, u32[]{:S(2)}) async-start(bf16[8,192,256]{2,1,0:T(8,128)(2,1)} %z_pack.1.refs_2_), calls=%async_computation.2 | async-start | bytes 1572864 | tf_op jit(solution)/shard_map/z_gather/all_to_all | solution.py:518
  46.3 6.4 %collective-permute-start.7 = (bf16[64,256]{1,0:T(8,128)(2,1)S(1)}, bf16[64,256]{1,0:T(8,128)(2,1)S(1)}, u32[]{:S(2)}, u32[]{:S(2)}) collective-permute-start(bf16[64,256]{1,0:T(8,128)(2,1)S(1)} %slice_bitcast_fusion), channel_id=1, source_target_pairs={{0,0},{1,1},{2,2},{3,3},{4,32},{5,33},{6,34},{7,35},{8,64},{9,65},... | collective-permute-start | bytes 98312 | tf_op jit(solution)/shard_map/z_gather/ppermute | solution.py:519
  52.7 14.1 %all_gather.3.refs_1_.refs_0_ = bf16[768,256]{1,0:T(8,128)(2,1)S(1)} all-gather(bf16[96,256]{1,0:T(8,128)(2,1)S(1)} %cols_pack.1), channel_id=1, replica_groups=mesh['row'=8,'col'=32] {'row'}, dimensions={0}, use_global_device_ids=true | all-gather | bytes 442368 | tf_op jit(solution)/shard_map/z_gather/all_gather | solution.py:527
  66.9 1.2 %all-to-all-done.2.refs_0_ = bf16[8,192,256]{2,1,0:T(8,128)(2,1)S(1)} async-done(((bf16[8,192,256]{2,1,0:T(8,128)(2,1)}), bf16[8,192,256]{2,1,0:T(8,128)(2,1)S(1)}, u32[]{:S(2)}, u32[]{:S(2)}) %all-to-all-start.2) | async-done | bytes 786464 | tf_op jit(solution)/shard_map/z_gather/all_to_all | solution.py:518
  69.8 9.5 %all-to-all-start.3 = ((bf16[8,128,256]{2,1,0:T(8,128)(2,1)}), bf16[8,128,256]{2,1,0:T(8,128)(2,1)S(1)}, u32[]{:S(2)}, u32[]{:S(2)}) async-start(bf16[8,128,256]{2,1,0:T(8,128)(2,1)} %row_pack.1), calls=%async_computation.3 | async-start | bytes 1048576 | tf_op jit(solution)/shard_map/row_gather/all_to_all | solution.py:539
  79.4 2.0 %collective-permute-start.10 = (bf16[1024,256]{1,0:T(8,128)(2,1)}, bf16[1024,256]{1,0:T(8,128)(2,1)S(1)}, u32[]{:S(2)}, u32[]{:S(2)}) collective-permute-start(bf16[1024,256]{1,0:T(8,128)(2,1)} %copy-done.4), channel_id=1, source_target_pairs={{0,2},{1,3},{2,0},{3,1},{4,6},{5,7},{6,4},{7,5},{8,10},{9,11},{10,... | collective-permute-start | bytes 1572872 | tf_op jit(solution)/shard_map/parts_over_y/ppermute | solution.py:547
  81.4 2.2 %collective-permute-start.9 = (bf16[1024,256]{1,0:T(8,128)(2,1)}, bf16[1024,256]{1,0:T(8,128)(2,1)}, u32[]{:S(2)}, u32[]{:S(2)}) collective-permute-start(bf16[1024,256]{1,0:T(8,128)(2,1)} %copy-done.4), channel_id=1, source_target_pairs={{0,3},{1,0},{2,1},{3,2},{4,7},{5,4},{6,5},{7,6},{8,11},{9,8},{10,9... | collective-permute-start | bytes 1572872 | tf_op jit(solution)/shard_map/parts_over_y/ppermute | solution.py:547
  83.5 3.5 %all-to-all-done.3.refs_1_ = bf16[8,128,256]{2,1,0:T(8,128)(2,1)S(1)} async-done(((bf16[8,128,256]{2,1,0:T(8,128)(2,1)}), bf16[8,128,256]{2,1,0:T(8,128)(2,1)S(1)}, u32[]{:S(2)}, u32[]{:S(2)}) %all-to-all-start.3) | async-done | bytes 524320 | tf_op jit(solution)/shard_map/row_gather/all_to_all | solution.py:539
  87.1 13.7 %factor.1 = (bf16[512,256]{1,0:T(8,128)(2,1)S(1)}, f32[256,256]{1,0:T(8,128)S(1)}, f32[256,256]{1,0:T(8,128)S(1)}, bf16[512,256]{1,0:T(8,128)(2,1)S(1)}) custom-call(bf16[256,768]{1,0:T(8,128)(2,1)S(1)} %get-tuple-element.31.x_ref.x_all_ref, bf16[256,256]{1,0:T(8,128)(2,1)S(1)} %get-tuple-element.32.old_ref, bf16[256,256]{1,0:T(8,128)(2,1)S(1)} %get-tuple-element.33.grad_ref), custom_call_target="tpu_custom_call" | custom-call | flops 16000000000 | bytes 1310720 | tf_op jit(solution)/shard_map/factor/factor/pallas_call | solution.py:198
  102.2 3.0 %rows.2 = (bf16[2048,512]{1,0:T(8,128)(2,1)}, f32[2048,512]{1,0:T(8,128)}, f32[2048,256]{1,0:T(8,128)}) custom-call(s32[1]{0:T(128)S(1)} %bitcast.9, bf16[2048,512]{1,0:T(8,128)(2,1)S(1)} %copy-done, f32[32,512]{1,0:T(8,128)S(1)} %copy-done.3, bf16[2048,256]{1,0:T(8,128)(2,1)S(1)} %copy-done.1, bf16[256,768]{1,0:T(8,128)(2,1)S(1)} %get-tuple-element.31.x_ref.x_all_ref, ...), custom_call_target="tpu_custom_call" | custom-call | flops 671088640 | bytes 3670016 | tf_op jit(solution)/shard_map/rows/rows/pallas_call | solution.py:324
  105.3 1.0 collective-permute-done.8.refs_0_
  106.3 8.5 %rows.3 = (bf16[2048,512]{1,0:T(8,128)(2,1)}, f32[2048,512]{1,0:T(8,128)}, f32[2048,256]{1,0:T(8,128)}) custom-call(s32[3]{0:T(128)S(1)} %slice.12.at_ref, bf16[2048,512]{1,0:T(8,128)(2,1)S(1)} %copy-done, f32[32,512]{1,0:T(8,128)S(1)} %copy-done.3, bf16[2048,256]{1,0:T(8,128)(2,1)S(1)} %copy-done.1, ...), custom_call_target="tpu_custom_call", output_to_operand_aliasing={{0}: (12, {}), {1}: (13, {}), {2}: (14, {})} | custom-call | flops 2013265920 | bytes 11010048 | tf_op jit(solution)/shard_map/rows/rows/pallas_call | solution.py:324
  (41 shorter events, 6.9 us)
Async XLA Ops:
  0.6 8.4 %copy-start.2 = (f32[32,512]{1,0:T(8,128)S(1)}, f32[32,512]{1,0:T(8,128)}, u32[]{:S(2)}) copy-start(f32[32,512]{1,0:T(8,128)} %scales_ref.7) | copy-start | bytes 196612
  0.6 8.4 %copy-start = (bf16[2048,512]{1,0:T(8,128)(2,1)S(1)}, bf16[2048,512]{1,0:T(8,128)(2,1)}, u32[]{:S(2)}) copy-start(bf16[2048,512]{1,0:T(8,128)(2,1)} %codes_ref.7) | copy-start | bytes 6291460
  3.0 20.3 %all-to-all-start = ((bf16[8,32,1024]{2,1,0:T(8,128)(2,1)}), bf16[8,32,1024]{2,1,0:T(8,128)(2,1)S(1)}, u32[]{:S(2)}, u32[]{:S(2)}) async-start(bf16[8,32,1024]{2,1,0:T(8,128)(2,1)} %bitcast.10), calls=%async_computation | async-start | bytes 1048576 | tf_op jit(solution)/shard_map/row_scatter/all_to_all | solution.py:495
  9.3 7.7 %collective-permute-start = (bf16[512,256]{1,0:T(8,128)(2,1)S(1)}, bf16[512,256]{1,0:T(8,128)(2,1)S(1)}, u32[]{:S(2)}, u32[]{:S(2)}) collective-permute-start(bf16[512,256]{1,0:T(8,128)(2,1)S(1)} %get-tuple-element.24), channel_id=1, source_target_pairs={{0,1},{32,33},{64,65},{96,97},{128,129},{160,161},{192,193},{224,2... | collective-permute-start | bytes 786440 | tf_op jit(solution)/shard_map/old_to_y/ppermute | solution.py:484
  11.6 10.9 %collective-permute-start.1 = (bf16[512,256]{1,0:T(8,128)(2,1)S(1)}, bf16[512,256]{1,0:T(8,128)(2,1)S(1)}, u32[]{:S(2)}, u32[]{:S(2)}) collective-permute-start(bf16[512,256]{1,0:T(8,128)(2,1)S(1)} %get-tuple-element.25), channel_id=1, source_target_pairs={{0,2},{32,34},{64,66},{96,98},{128,130},{160,162},{192,194},{224,2... | collective-permute-start | bytes 786440 | tf_op jit(solution)/shard_map/old_to_y/ppermute | solution.py:484
  13.9 8.6 %collective-permute-start.2 = (bf16[512,256]{1,0:T(8,128)(2,1)S(1)}, bf16[512,256]{1,0:T(8,128)(2,1)S(1)}, u32[]{:S(2)}, u32[]{:S(2)}) collective-permute-start(bf16[512,256]{1,0:T(8,128)(2,1)S(1)} %get-tuple-element.26), channel_id=1, source_target_pairs={{0,3},{32,35},{64,67},{96,99},{128,131},{160,163},{192,195},{224,2... | collective-permute-start | bytes 786440 | tf_op jit(solution)/shard_map/old_to_y/ppermute | solution.py:484
  23.3 18.5 %all-to-all-start.1 = ((bf16[8,64,256]{2,1,0:T(8,128)(2,1)}), bf16[8,64,256]{2,1,0:T(8,128)(2,1)S(1)}, u32[]{:S(2)}, u32[]{:S(2)}) async-start(bf16[8,64,256]{2,1,0:T(8,128)(2,1)} %bitcast.2), calls=%async_computation.1 | async-start | bytes 524288 | tf_op jit(solution)/shard_map/old_to_z/all_to_all | solution.py:504
  26.8 14.0 %collective-permute-start.3 = (bf16[32,512]{1,0:T(8,128)(2,1)S(1)}, bf16[32,512]{1,0:T(8,128)(2,1)S(1)}, u32[]{:S(2)}, u32[]{:S(2)}) collective-permute-start(bf16[32,512]{1,0:T(8,128)(2,1)S(1)} %get-tuple-element.28.refs_1_), channel_id=1, source_target_pairs={{0,0},{1,1},{2,2},{3,3},{4,32},{5,33},{6,34},{7,35},{8,64},{9,65},... | collective-permute-start | bytes 98312 | tf_op jit(solution)/shard_map/swap_samples/ppermute | solution.py:510
  32.4 0.6 copy-start.6
  33.1 19.6 %copy-start.7 = (bf16[32,512]{1,0:T(8,128)(2,1)S(1)}, bf16[32,512]{1,0:T(8,128)(2,1)}, u32[]{:S(2)}) copy-start(bf16[32,512]{1,0:T(8,128)(2,1)} %copy-done.6) | copy-start | bytes 98308
  33.1 7.7 %collective-permute-start.6 = (bf16[64,256]{1,0:T(8,128)(2,1)S(1)}, bf16[64,256]{1,0:T(8,128)(2,1)S(1)}, u32[]{:S(2)}, u32[]{:S(2)}) collective-permute-start(bf16[64,256]{1,0:T(8,128)(2,1)S(1)} %get-tuple-element.29.refs_2_), channel_id=1, source_target_pairs={{0,3},{32,35},{64,67},{96,99},{128,131},{160,163},{192,195},{224,2... | collective-permute-start | bytes 98312 | tf_op jit(solution)/shard_map/slices_to_y/ppermute | solution.py:508
  36.9 3.9 %collective-permute-start.5 = (bf16[64,256]{1,0:T(8,128)(2,1)S(1)}, bf16[64,256]{1,0:T(8,128)(2,1)S(1)}, u32[]{:S(2)}, u32[]{:S(2)}) collective-permute-start(bf16[64,256]{1,0:T(8,128)(2,1)S(1)} %get-tuple-element.29.refs_2_), channel_id=1, source_target_pairs={{0,2},{32,34},{64,66},{96,98},{128,130},{160,162},{192,194},{224,2... | collective-permute-start | bytes 98312 | tf_op jit(solution)/shard_map/slices_to_y/ppermute | solution.py:508
  39.5 2.3 %collective-permute-start.4 = (bf16[64,256]{1,0:T(8,128)(2,1)S(1)}, bf16[64,256]{1,0:T(8,128)(2,1)S(1)}, u32[]{:S(2)}, u32[]{:S(2)}) collective-permute-start(bf16[64,256]{1,0:T(8,128)(2,1)S(1)} %get-tuple-element.29.refs_2_), channel_id=1, source_target_pairs={{0,1},{32,33},{64,65},{96,97},{128,129},{160,161},{192,193},{224,2... | collective-permute-start | bytes 98312 | tf_op jit(solution)/shard_map/slices_to_y/ppermute | solution.py:508
  42.7 25.3 %all-to-all-start.2 = ((bf16[8,192,256]{2,1,0:T(8,128)(2,1)}), bf16[8,192,256]{2,1,0:T(8,128)(2,1)S(1)}, u32[]{:S(2)}, u32[]{:S(2)}) async-start(bf16[8,192,256]{2,1,0:T(8,128)(2,1)} %z_pack.1.refs_2_), calls=%async_computation.2 | async-start | bytes 1572864 | tf_op jit(solution)/shard_map/z_gather/all_to_all | solution.py:518
  46.3 20.6 %collective-permute-start.7 = (bf16[64,256]{1,0:T(8,128)(2,1)S(1)}, bf16[64,256]{1,0:T(8,128)(2,1)S(1)}, u32[]{:S(2)}, u32[]{:S(2)}) collective-permute-start(bf16[64,256]{1,0:T(8,128)(2,1)S(1)} %slice_bitcast_fusion), channel_id=1, source_target_pairs={{0,0},{1,1},{2,2},{3,3},{4,32},{5,33},{6,34},{7,35},{8,64},{9,65},... | collective-permute-start | bytes 98312 | tf_op jit(solution)/shard_map/z_gather/ppermute | solution.py:519
  52.7 26.6 %copy-start.8 = (s32[4]{0:T(128)S(1)}, s32[4]{0:T(128)}, u32[]{:S(2)}) copy-start(s32[4]{0:T(128)} %constant.29) | copy-start | bytes 52
  68.1 0.8 copy-start.4
  69.8 17.3 %all-to-all-start.3 = ((bf16[8,128,256]{2,1,0:T(8,128)(2,1)}), bf16[8,128,256]{2,1,0:T(8,128)(2,1)S(1)}, u32[]{:S(2)}, u32[]{:S(2)}) async-start(bf16[8,128,256]{2,1,0:T(8,128)(2,1)} %row_pack.1), calls=%async_computation.3 | async-start | bytes 1048576 | tf_op jit(solution)/shard_map/row_gather/all_to_all | solution.py:539
  79.4 25.9 %collective-permute-start.10 = (bf16[1024,256]{1,0:T(8,128)(2,1)}, bf16[1024,256]{1,0:T(8,128)(2,1)S(1)}, u32[]{:S(2)}, u32[]{:S(2)}) collective-permute-start(bf16[1024,256]{1,0:T(8,128)(2,1)} %copy-done.4), channel_id=1, source_target_pairs={{0,2},{1,3},{2,0},{3,1},{4,6},{5,7},{6,4},{7,5},{8,10},{9,11},{10,... | collective-permute-start | bytes 1572872 | tf_op jit(solution)/shard_map/parts_over_y/ppermute | solution.py:547
  81.4 23.9 %collective-permute-start.9 = (bf16[1024,256]{1,0:T(8,128)(2,1)}, bf16[1024,256]{1,0:T(8,128)(2,1)}, u32[]{:S(2)}, u32[]{:S(2)}) collective-permute-start(bf16[1024,256]{1,0:T(8,128)(2,1)} %copy-done.4), channel_id=1, source_target_pairs={{0,3},{1,0},{2,1},{3,2},{4,7},{5,4},{6,5},{7,6},{8,11},{9,8},{10,9... | collective-permute-start | bytes 1572872 | tf_op jit(solution)/shard_map/parts_over_y/ppermute | solution.py:547
  83.5 22.8 %collective-permute-start.8 = (bf16[1024,256]{1,0:T(8,128)(2,1)}, bf16[1024,256]{1,0:T(8,128)(2,1)}, u32[]{:S(2)}, u32[]{:S(2)}) collective-permute-start(bf16[1024,256]{1,0:T(8,128)(2,1)} %copy-done.4), channel_id=1, source_target_pairs={{0,1},{1,2},{2,3},{3,0},{4,5},{5,6},{6,7},{7,4},{8,9},{9,10},{10,1... | collective-permute-start | bytes 1572872 | tf_op jit(solution)/shard_map/parts_over_y/ppermute | solution.py:547
  100.8 1.2 %copy-start.1 = (bf16[2048,256]{1,0:T(8,128)(2,1)S(1)}, bf16[2048,256]{1,0:T(8,128)(2,1)}, u32[]{:S(2)}) copy-start(bf16[2048,256]{1,0:T(8,128)(2,1)} %grad_ref.5) | copy-start | bytes 3145732
  100.9 1.2 %copy-start.3 = (f32[32,512]{1,0:T(8,128)S(1)}, f32[32,512]{1,0:T(8,128)}, u32[]{:S(2)}) copy-start(f32[32,512]{1,0:T(8,128)} %scales_ref.7) | copy-start | bytes 196612
  100.9 1.4 %copy-start.5 = (bf16[1024,256]{1,0:T(8,128)(2,1)S(1)}, bf16[1024,256]{1,0:T(8,128)(2,1)}, u32[]{:S(2)}) copy-start(bf16[1024,256]{1,0:T(8,128)(2,1)} %copy-done.4) | copy-start | bytes 1572868
